TPU v7x, 32 devices: a whole 2x2x4 slice. The times are simulated.
32 devices in a mesh: members: 2 (over y), wave: 4 (over z), lev: 2 (over x), fld: 2 (over core).
Axes of the slice: x: 2, y: 2, z: 4, core: 2. Of those that a mesh axis runs over, the one named last changes fastest.
Arguments:
- spec_main: bfloat16 [4, 96, 384, 1536], P(('members', 'fld'), 'lev', 'wave'), parts along dimension 0, may hold values from -6 to 6
- spec_diag: bfloat16 [4, 96, 768], P(('members', 'fld'), 'lev', 'wave'), parts along dimension 0, may hold values from -6 to 6
- pair_slots: int32 [384], P('wave'), may hold values from 0 to 383, each once
- correlation: bfloat16 [384, 2, 2, 96, 96], P(('wave', 'lev'), None, 'fld'), may hold values from -0.625 to 0.625
- balance: bfloat16 [384, 2, 96, 96], P(('wave', 'lev')), may hold values from -0.625 to 0.625
- legendre: bfloat16 [384, 32, 768], P('wave'), may hold values from -0.01171875 to 0.01171875
- legendre_diag: bfloat16 [384, 32], P('wave'), may hold values from -0.21875 to 0.21875
Outputs:
- grid_fields: float32 [4, 96, 32, 128], P(('members', 'fld'), 'lev', 'wave'), parts along dimension 0
There are 2 independent parts, one for each index of `members`. A program takes and returns all parts, laid end to end along the dimension named above; an argument that names none is the same for every part. Nothing has to cross between parts.
Inputs may be any that keep to these rules, and one draw needn't show every extreme that they name: pair_slots holds every pair once: slot r carries the orders pair_slots[r] and 767 - pair_slots[r].
All inputs are finite; a program needn't handle non-finite values.
Results may differ from a plain program's by a relative error of at most 0.0034.
Values may be sent and summed in bfloat16 or wider, within the bound.
A program may use at most 256 MiB of HBM per device.

v0:
```python
import math

import jax
import jax.numpy as jnp
from jax import lax
from jax.sharding import PartitionSpec as P

NWAVE = 768
NLON = 128


def passed_along(value, axis, steps):
    count = lax.axis_size(axis)
    initial, last = (max(0, -steps), min(count, count - steps))
    return lax.ppermute(value, axis, [(source, source + steps) for source in range(initial, last)])


def order_table(orders, length):
    columns = jnp.arange(length, dtype=jnp.int32)
    phases = orders[..., None] * columns % (2 * NWAVE)
    angles = phases.astype(jnp.float32) * (math.pi / NWAVE)
    weight = jnp.where(orders == 0, 1.0, 2.0).astype(jnp.float32)[..., None]
    return jnp.stack([weight * jnp.cos(angles), -weight * jnp.sin(angles)], axis=-2)


def correlate(matrices, values, second, lower_mask):
    upper_part = jnp.einsum(
        "bkl,lrbsc->krbsc", matrices[:, 1], values, preferred_element_type=jnp.float32
    )
    lower_part = jnp.einsum(
        "bkl,lrbc->krbc", matrices[:, 0], values[:, :, :, 1], preferred_element_type=jnp.float32
    )
    picked = second & lower_mask[None, :, :, None, None]
    return jnp.where(picked, lower_part[:, :, :, None, :], upper_part)


def body(spec_main, spec_diag, pair_slots, correlation, balance, legendre, legendre_diag):
    level_part = spec_main.shape[1]
    slot_rows = spec_main.shape[2]
    pair_count = spec_main.shape[3] // 4
    here_pairs = correlation.shape[0]
    wave_count = lax.axis_size("wave")
    lev_count = lax.axis_size("lev")
    owner_count = wave_count * lev_count
    block_width = here_pairs * 4
    orders_all = lax.all_gather(pair_slots, "wave", axis=0, tiled=True)
    first_pair = (lax.axis_index("wave") * lev_count + lax.axis_index("lev")) * here_pairs
    pair_ids = first_pair + jnp.arange(here_pairs, dtype=jnp.int32)
    lower_mask = pair_ids[None, :] >= orders_all[:, None]
    chosen = (orders_all[:, None] == pair_ids[None, :]).astype(jnp.bfloat16)
    pair_range = jnp.arange(pair_count, dtype=jnp.int32)
    onehot = (pair_range[None, :] == pair_slots[:, None]).astype(jnp.bfloat16)
    arrived = lax.all_to_all(
        lax.all_to_all(spec_main, "wave", split_axis=3, concat_axis=2, tiled=True),
        "lev",
        split_axis=3,
        concat_axis=1,
        tiled=True,
    )
    full_levels = arrived.shape[1]
    all_rows = arrived.shape[2]
    arrived = arrived.reshape(full_levels, all_rows, block_width)
    gathered_diag = lax.all_gather(spec_diag, ("wave", "lev"), axis=0, tiled=True)
    gathered_diag = gathered_diag.reshape(wave_count, lev_count, level_part, slot_rows, 2)
    pieces = gathered_diag.transpose(1, 2, 0, 3, 4).reshape(full_levels, all_rows, 2)
    diag_here = jnp.einsum(
        "krc,rb->bkc", pieces, chosen, preferred_element_type=jnp.float32
    ).astype(jnp.bfloat16)
    values = arrived.reshape(full_levels, all_rows, here_pairs, 2, 2)
    second = (jnp.arange(2) == 1)[None, None, None, :, None]
    correlated = correlate(correlation[:, :, 0], values, second, lower_mask)
    sent_field = correlated.astype(jnp.bfloat16)
    diag_corr = jnp.einsum(
        "bkl,blc->bkc", correlation[:, 1, 0], diag_here, preferred_element_type=jnp.float32
    )
    diag_sent = diag_corr.astype(jnp.bfloat16)
    received, diag_received = passed_along((sent_field, diag_sent), "fld", 1)
    coupled = correlate(balance, received, second, lower_mask)
    balanced = (correlated + coupled).astype(jnp.bfloat16)
    diag_coupled = jnp.einsum(
        "bkl,blc->bkc", balance[:, 1], diag_received, preferred_element_type=jnp.float32
    )
    diag_balanced = (diag_corr + diag_coupled).astype(jnp.bfloat16)
    main_out = balanced.reshape(full_levels, all_rows, block_width)
    outgoing = main_out
    outgoing = outgoing.reshape(1, full_levels, all_rows, 1, 1, block_width)
    returned = lax.all_to_all(
        lax.all_to_all(outgoing, "wave", split_axis=2, concat_axis=3, tiled=True),
        "lev",
        split_axis=1,
        concat_axis=4,
        tiled=True,
    )
    returned = returned.reshape(level_part, slot_rows, owner_count, block_width)
    main_values = returned.reshape(level_part, slot_rows, pair_count, 2, 2)
    gathered = lax.all_gather(diag_balanced, ("wave", "lev"), axis=0, tiled=True)
    own_levels = lax.dynamic_slice_in_dim(
        gathered, lax.axis_index("lev") * level_part, level_part, 1
    )
    diag_values = jnp.einsum("bkc,rb->krc", own_levels, onehot, preferred_element_type=jnp.float32)
    lat_count = legendre.shape[1]
    tables = legendre.reshape(slot_rows, lat_count, pair_count, 2)
    own_lower = pair_range[None, :] >= pair_slots[:, None]
    slot_second = (jnp.arange(2) == 1)[None, None, None, :]
    keep_first = jnp.logical_or(jnp.logical_not(slot_second), own_lower[:, None, :, None])
    keep_second = jnp.logical_and(slot_second, jnp.logical_not(own_lower)[:, None, :, None])
    nothing = jnp.zeros_like(tables)
    stacked = jnp.stack(
        [jnp.where(keep_first, tables, nothing), jnp.where(keep_second, tables, nothing)], axis=1
    )
    coeffs = jnp.einsum(
        "rijbs,krbsc->jkric", stacked, main_values, preferred_element_type=jnp.float32
    )
    sectoral = legendre_diag.T.astype(jnp.float32)[:, None, :, None] * diag_values[None]
    order_second = (jnp.arange(2) == 1).astype(jnp.float32)[None, None, None, :, None]
    coeffs = coeffs + sectoral[:, :, :, None, :] * order_second
    flattened = coeffs.reshape(lat_count, level_part, slot_rows * 4)
    own_orders = jnp.stack([pair_slots, NWAVE - 1 - pair_slots], axis=1)
    fourier_table = order_table(own_orders, NLON).reshape(slot_rows * 4, NLON)
    banded = lax.psum_scatter(
        jnp.einsum(
            "jkq,ql->jkl",
            flattened,
            fourier_table,
            precision=lax.Precision.HIGHEST,
            preferred_element_type=jnp.float32,
        ),
        "wave",
        scatter_dimension=0,
        tiled=True,
    )
    return banded.transpose(1, 0, 2)[None]


def solution(mesh):
    return jax.shard_map(
        body,
        mesh=mesh,
        in_specs=(
            P(("members", "fld"), "lev", "wave", None),
            P(("members", "fld"), "lev", "wave"),
            P("wave"),
            P(("wave", "lev"), None, "fld", None, None),
            P(("wave", "lev"), None, None, None),
            P("wave", None, None),
            P("wave", None),
        ),
        out_specs=P(("members", "fld"), "lev", "wave", None),
        check_vma=False,
    )
```

profile of v0, /device:TPU:0, one launch (start us, length us, event | category | flops | bytes accessed | tf_op | source)
XLA Modules:
  0.0 1702.3 jit_solution(5235264751605589770)
XLA Ops:
  6.5 22.6 %copy.47 = bf16[1,48,96,1536]{2,1,0,3:T(8,128)(2,1)} copy(bf16[1,48,96,1536]{3,2,1,0:T(8,128)(2,1)} %param.7) | data formatting | bytes 28311552 | tf_op args[0]
  29.1 421.5 %all_to_all.66 = bf16[1,48,96,1536]{2,1,0,3:T(8,128)(2,1)} all-to-all(bf16[1,48,96,1536]{2,1,0,3:T(8,128)(2,1)} %copy.47), channel_id=1, replica_groups=mesh['members'=2,'wave'=4,'lev'=2,'fld'=2] {'wave'}, dimensions={3} | all-to-all | bytes 28311552 | tf_op jit(solution)/shard_map/all_to_all | solution.py:54
  450.6 23.5 %copy.81 = bf16[1,48,96,4,384]{4,3,2,1,0:T(4,128)(2,1)} copy(bf16[1,48,96,4,384]{2,1,4,3,0:T(8,128)(2,1)} %bitcast.147) | data formatting | bytes 28311552 | tf_op jit(solution)/shard_map/all_to_all | solution.py:54
  474.1 14.0 copy.49
  488.1 18.6 %copy.50 = bf16[1,48,384,384]{2,1,0,3:T(8,128)(2,1)} copy(bf16[1,48,384,384]{3,2,1,0:T(8,128)(2,1)} %bitcast.149) | data formatting | bytes 28311552 | tf_op jit(solution)/shard_map/all_to_all | solution.py:54
  506.7 0.0 copy-start.6
  506.7 9.0 all-to-all-start.1
  515.7 1.8 copy.98
  517.6 0.0 copy-done.6
  517.6 0.6 dynamic-slice
  518.8 0.0 copy-done.5
  518.8 0.2 dynamic-update-slice
  519.1 5.6 all-reduce
  524.7 0.1 broadcast_compare_fusion
  524.7 0.1 broadcast_and_fusion.1
  524.9 144.6 %all-to-all-done.1 = bf16[1,48,384,384]{2,1,0,3:T(8,128)(2,1)} async-done(((bf16[1,48,384,384]{2,1,0,3:T(8,128)(2,1)}), bf16[1,48,384,384]{2,1,0,3:T(8,128)(2,1)}, u32[]{:S(2)}, u32[]{:S(2)}) %all-to-all-start.1) | async-done | bytes 14155808 | tf_op jit(solution)/shard_map/all_to_all | solution.py:53
  669.5 9.2 copy.51
  678.8 35.8 %copy.52 = bf16[1,2,48,384,192]{3,2,1,4,0:T(8,128)(2,1)S(1)} copy(bf16[1,2,48,384,192]{3,4,1,2,0:T(8,128)(2,1)S(1)} %bitcast.150) | data formatting | bytes 28311552 | tf_op jit(solution)/shard_map/all_to_all | solution.py:53
  714.6 0.0 copy-start
  714.6 4.9 copy-done
  719.5 7.0 convolution_bitcast_fusion.1
  726.5 23.3 %fusion.2 = (bf16[96,384,48,2,2]{1,0,4,3,2:T(8,128)(2,1)}, f32[48,384,2,2,96]{1,4,3,2,0:T(8,128)}) fusion(f32[96,384,48,2]{1,0,3,2:T(8,128)} %convolution_bitcast_fusion.1, pred[384,48,2]{0,2,1:T(4,128)(4,1)S(1)} %broadcast_and_fusion.1, bf16[96,384,48,2,2]{1,0,4,3,2:T(8,128)(2,1)} %bitcast.143, bf16[48,2,96,96]{3,2,0,1:T(8,128)(2,1)S(1)} %bitcast.154), kind=kOutput, calls=%fused_computation.4 | convolution fusion | flops 1366032384 | bytes 72032256 | tf_op jit(solution)/shard_map/bkl,lrbsc->krbsc/dot_general | solution.py:27
  749.8 2.5 collective-permute-start
  752.3 20.1 %collective-permute-done = bf16[96,384,48,2,2]{1,0,4,3,2:T(8,128)(2,1)S(1)} collective-permute-done((bf16[96,384,48,2,2]{1,0,4,3,2:T(8,128)(2,1)}, bf16[96,384,48,2,2]{1,0,4,3,2:T(8,128)(2,1)S(1)}, u32[]{:S(2)}, u32[]{:S(2)}) %collective-permute-start) | collective-permute-done | bytes 14155808 | tf_op jit(solution)/shard_map/ppermute | solution.py:15
  772.4 9.2 convolution_bitcast_fusion
  781.6 0.2 copy-done.1
  781.8 0.0 copy-done.2
  781.8 28.6 %fusion.1 = bf16[96,384,48,2,2]{1,0,4,3,2:T(8,128)(2,1)} fusion(f32[48,384,2,2,96]{1,4,3,2,0:T(8,128)} %get-tuple-element.14, f32[96,384,48,2]{1,0,3,2:T(8,128)} %convolution_bitcast_fusion, f32[96,384,48,2]{1,0,3,2:T(8,128)} %convolution_bitcast_fusion.1, pred[384,48,2]{0,2,1:T(4,128)(4,1)S(1)} %broadcast_and_fusion.1, ...), kind=kOutput, calls=%fused_computation.2 | convolution fusion | flops 1387266048 | bytes 86188032 | tf_op jit(solution)/shard_map/bkl,lrbsc->krbsc/dot_general | solution.py:27
  810.4 22.6 %copy.57 = bf16[1,96,384,1,1,192]{1,5,4,3,0,2:T(8,128)(2,1)} copy(bf16[1,96,384,1,1,192]{2,1,5,4,3,0:T(8,128)(2,1)} %bitcast.144) | data formatting | bytes 28311552 | tf_op jit(solution)/shard_map/reshape;reshape | solution.py:86
  833.0 420.6 %all_to_all.67 = bf16[1,96,384,1,1,192]{1,5,4,3,0,2:T(8,128)(2,1)} all-to-all(bf16[1,96,384,1,1,192]{1,5,4,3,0,2:T(8,128)(2,1)} %copy.57), channel_id=1, replica_groups=mesh['members'=2,'wave'=4,'lev'=2,'fld'=2] {'wave'}, dimensions={2} | all-to-all | bytes 28311552 | tf_op jit(solution)/shard_map/all_to_all | solution.py:88
  1253.5 31.7 %copy.58 = bf16[1,96,4,96,1,1,192]{6,3,2,1,5,4,0:T(8,128)(2,1)} copy(bf16[1,96,4,96,1,1,192]{1,6,3,2,5,4,0:T(8,128)(2,1)} %bitcast.146) | data formatting | bytes 28311552 | tf_op jit(solution)/shard_map/all_to_all | solution.py:88
  1285.2 10.7 all-to-all-start.3
  1295.9 0.0 reduce-scatter.2.cloned.1.call-start
  1296.0 0.0 copy-done.3
  1296.0 228.6 %all_gather.10 = bf16[8,48,192]{2,1,0:T(8,128)(2,1)S(1)} all-gather(bf16[1,48,192]{2,1,0:T(8,128)(2,1)S(1)} %copy-done.3), channel_id=1, replica_groups=mesh['members'=2,'wave'=4,'lev'=2,'fld'=2] {'wave','lev'}, dimensions={0}, use_global_device_ids=true | all-gather | bytes 165888 | tf_op jit(solution)/shard_map/all_gather | solution.py:63
  1524.6 0.2 copy.65
  1524.8 0.4 copy.66
  1525.2 0.2 reshape.221
  1525.4 0.2 convolution_convert_fusion
  1525.6 2.0 fusion.16
  1527.6 1.3 collective-permute-start.1
  1528.9 9.3 copy.60
  1538.3 9.4 copy.61
  1547.7 0.0 copy-done.4
  1547.7 0.1 iota_compare_fusion.1
  1547.8 0.5 cosine_multiply_fusion
  1548.3 0.4 broadcast_and_fusion
  1548.8 7.4 broadcast_select_fusion.1
  1556.2 0.1 copy.64
  1556.3 0.0 collective-permute-done.1
  1556.3 0.7 fusion.26
  1557.0 31.0 %all_gather.11 = bf16[384,96,2]{1,2,0:T(2,128)(2,1)S(1)} all-gather(bf16[48,96,2]{1,2,0:T(2,128)(2,1)S(1)} %fusion.26), channel_id=1, replica_groups=mesh['members'=2,'wave'=4,'lev'=2,'fld'=2] {'wave','lev'}, dimensions={0}, use_global_device_ids=true | all-gather | bytes 165888 | tf_op jit(solution)/shard_map/all_gather | solution.py:96
  1588.0 0.3 constant_dynamic-slice_fusion
  1588.3 0.3 convolution_bitcast_fusion.2
  1588.6 0.1 copy.70
  1588.7 0.5 broadcast_multiply_fusion
  1589.2 0.0 all-to-all-done.3
  1589.2 26.7 %copy.59 = bf16[1,48,96,4,2,1,192]{2,1,6,4,3,5,0:T(8,128)(2,1)} copy(bf16[1,48,96,4,2,1,192]{6,2,5,3,1,4,0:T(8,128)(2,1)} %bitcast.31) | data formatting | bytes 28311552 | tf_op jit(solution)/shard_map/all_to_all | solution.py:87
  1615.9 25.7 %copy.77 = bf16[48,96,384,2,2,1]{2,0,3,5,4,1:T(8,128)(2,1)} copy(bf16[48,96,384,2,2,1]{1,0,4,3,2,5:T(8,128)(2,1)} %bitcast.148) | data formatting | bytes 28311552 | tf_op jit(solution)/shard_map/reshape;reshape | solution.py:95
  1641.6 14.5 bitcast_add_fusion
  1656.1 16.3 fusion.8
  1672.3 0.0 reduce-scatter.2.cloned.1.call-update
  1672.4 21.4 %reduce-scatter.2.cloned.1.call-done = f32[8,48,128]{2,1,0:T(8,128)} async-done(((f32[32,48,128]{2,1,0:T(8,128)}), f32[8,48,128]{2,1,0:T(8,128)}) %reduce-scatter.2.cloned.1.call-update) | async-done | bytes 196624 | tf_op jit(solution)/shard_map/reduce_scatter | solution.py:120
  1693.8 1.7 copy.72
  (15 shorter events, 0.1 us)
Async XLA Ops:
  506.7 10.9 copy-start.6
  506.7 12.2 copy-start.5
  506.7 162.9 %all-to-all-start.1 = ((bf16[1,48,384,384]{2,1,0,3:T(8,128)(2,1)}), bf16[1,48,384,384]{2,1,0,3:T(8,128)(2,1)}, u32[]{:S(2)}, u32[]{:S(2)}) async-start(bf16[1,48,384,384]{2,1,0,3:T(8,128)(2,1)} %copy.50), calls=%async_computation.1 | async-start | bytes 28311552 | tf_op jit(solution)/shard_map/all_to_all | solution.py:53
  714.6 4.9 copy-start
  749.8 32.0 %copy-start.2 = (bf16[48,2,96,96]{3,2,1,0:T(8,128)(2,1)S(1)}, bf16[48,2,96,96]{3,2,1,0:T(8,128)(2,1)}, u32[]{:S(2)}) copy-start(bf16[48,2,96,96]{3,2,1,0:T(8,128)(2,1)} %param.11) | copy-start | bytes 5308420
  749.8 22.6 %collective-permute-start = (bf16[96,384,48,2,2]{1,0,4,3,2:T(8,128)(2,1)}, bf16[96,384,48,2,2]{1,0,4,3,2:T(8,128)(2,1)S(1)}, u32[]{:S(2)}, u32[]{:S(2)}) collective-permute-start(bf16[96,384,48,2,2]{1,0,4,3,2:T(8,128)(2,1)} %get-tuple-element.13), channel_id=1, source_target_pairs={{0,1},{2,3},{4,5},{6,7},{8,9},{10,11},{12,13},{14,15},{16,17},{18,... | collective-permute-start | bytes 42467336 | tf_op jit(solution)/shard_map/ppermute | solution.py:15
  772.4 9.4 copy-start.1
  1285.2 10.7 copy-start.3
  1285.2 304.0 %all-to-all-start.3 = ((bf16[1,96,96,4,1,192]{5,2,4,3,0,1:T(8,128)(2,1)}), bf16[1,96,96,4,1,192]{5,2,4,3,0,1:T(8,128)(2,1)}, u32[]{:S(2)}, u32[]{:S(2)}) async-start(bf16[1,96,96,4,1,192]{5,2,4,3,0,1:T(8,128)(2,1)} %bitcast.145), calls=%async_computation.3 | async-start | bytes 37748736 | tf_op jit(solution)/shard_map/all_to_all | solution.py:87
  1295.9 397.8 %reduce-scatter.2.cloned.1.call-start = ((), (), s32[]{:S(2)}) async-start(), calls=%async_computation.5 | async-start | bytes 983040 | tf_op jit(solution)/shard_map/reduce_scatter | solution.py:120
  1527.6 28.6 %collective-permute-start.1 = (bf16[48,96,2]{1,2,0:T(2,128)(2,1)S(1)}, bf16[48,96,2]{1,2,0:T(2,128)(2,1)S(1)}, u32[]{:S(2)}, u32[]{:S(2)}) collective-permute-start(bf16[48,96,2]{1,2,0:T(2,128)(2,1)S(1)} %convert_bitcast_fusion), channel_id=1, source_target_pairs={{0,1},{2,3},{4,5},{6,7},{8,9},{10,11},{12,13},{14,15},{16,17},{18,... | collective-permute-start | bytes 55304 | tf_op jit(solution)/shard_map/ppermute | solution.py:15
  1538.3 9.5 copy-start.4
Sparse Core Ops, SparseCore 0:
  1672.5 21.2 reduce-scatter.1
where the time goes:
time: 1710 us; the launch traced here: 1700 us
  blocking collectives  1110 us (65%)
  local copies, waits for them, and re-layouts  260 us (15%)
  waiting for transfers between devices  186 us (11%)
  matrix products  102 us (6%)
  starting transfers between devices  23.5 us (1%)
    all_to_all x1, blocking collectives, body(): lax.all_to_all(spec_main, 'wave', split_axis=3, concat_axis=2, tiled=True)  421 us
    all_to_all x1, blocking collectives, body(): lax.all_to_all(outgoing, 'wave', split_axis=2, concat_axis=3, tiled=True)  421 us
    all_gather x1, blocking collectives, body(): lax.all_gather(spec_diag, ('wave', 'lev'), axis=0, tiled=True)  229 us
    all_to_all x1, waiting for transfers between devices, body(): lax.all_to_all(lax.all_to_all(spec_main, 'wave', split_axis=3, concat_axi...  145 us
    all_to_all x3, local copies, waits for them, and re-layouts, body(): lax.all_to_all(spec_main, 'wave', split_axis=3, concat_axis=2, tiled=True)  56.1 us
    dot_general x2, matrix products, correlate(): jnp.einsum('bkl,lrbsc->krbsc', matrices[:, 1], values, preferred_element_...  51.9 us
    all_to_all x2, local copies, waits for them, and re-layouts, body(): lax.all_to_all(lax.all_to_all(spec_main, 'wave', split_axis=3, concat_axi...  45 us
    unnamed x20, local copies, waits for them, and re-layouts  39.7 us
  transfers between devices with their start and end apart: 5, of which 3 were waited for; matrix products, arithmetic and copies ran while one was open for 2% of the time, Pallas kernels for 0%

commit v1 on v0

v1 whole, which is shorter than its diff:
```python
import functools
import math

import jax
import jax.numpy as jnp
from jax import lax
from jax.experimental import pallas as pl
from jax.experimental.pallas import tpu as pltpu
from jax.sharding import PartitionSpec as P

NWAVE = 768
NLON = 128
STEP = 64
LANES = 128


def order_table(orders, length):
    columns = jnp.arange(length, dtype=jnp.int32)
    phases = orders[..., None] * columns % (2 * NWAVE)
    angles = phases.astype(jnp.float32) * (math.pi / NWAVE)
    weight = jnp.where(orders == 0, 1.0, 2.0).astype(jnp.float32)[..., None]
    return jnp.stack([weight * jnp.cos(angles), -weight * jnp.sin(angles)], axis=-2)


def synth_kernel(group, rows, levels, lats, ids_ref, low_ref, x_ref, xd_ref, w_ref, p_ref,
                 out_ref, diag_ref, ysc, acc):
    step = pl.program_id(0)
    steps = pl.num_programs(0)
    orders = jnp.concatenate([low_ref[...], low_ref[...]], axis=0)

    def unit_group(g, carry):
        for e in range(group):
            u = g * group + e
            w = w_ref[g]
            base = e * 2 * levels
            w_low = w[:, base:base + levels]
            w_up = w[:, base + levels:base + 2 * levels]
            first = x_ref[u, 0].reshape(2 * rows, x_ref.shape[-1])
            second = x_ref[u, 1].reshape(2 * rows, x_ref.shape[-1])
            y0 = jnp.dot(first, w_up, preferred_element_type=jnp.float32)
            y1u = jnp.dot(second, w_up, preferred_element_type=jnp.float32)
            y1l = jnp.dot(second, w_low, preferred_element_type=jnp.float32)
            diag_ref[u, :, 0:levels] = jnp.dot(xd_ref[u], w_up, preferred_element_type=jnp.float32)
            b = ids_ref[step * STEP + u]
            y1 = jnp.where(orders <= b, y1l, y1u)
            for c in range(2):
                for s, y in ((0, y0), (1, y1)):
                    ysc[c, pl.ds(2 * u + s, rows, stride=2 * STEP), 0:levels] = (
                        y[c * rows:(c + 1) * rows])
        return carry

    lax.fori_loop(0, STEP // group, unit_group, 0)

    @pl.when(step == 0)
    def _():
        acc[...] = jnp.zeros_like(acc)

    def slot(r, carry):
        start = pl.multiple_of(r * 2 * STEP, 2 * STEP)
        table = p_ref[r]
        for c in range(2):
            y = ysc[c, pl.ds(start, 2 * STEP), :].astype(jnp.bfloat16)
            acc[r, c] += jnp.dot(table, y, preferred_element_type=jnp.float32)
        return carry

    lax.fori_loop(0, rows, slot, 0)

    @pl.when(step == steps - 1)
    def _():
        def spread(r, carry):
            for c in range(2):
                for i in range(2):
                    out_ref[pl.ds(r * 4 + i * 2 + c, lats, stride=4 * rows), :] = (
                        acc[r, c, i * lats:(i + 1) * lats])
            return carry

        lax.fori_loop(0, rows, spread, 0)


def synthesize(ids, low, x, xd, w, tables, levels):
    units, _, _, rows, part = x.shape
    lats = tables.shape[1] // 2
    group = w.shape[-1] // (2 * levels)
    steps = units // STEP
    return pl.pallas_call(
        functools.partial(synth_kernel, group, rows, levels, lats),
        grid=(steps,),
        in_specs=[
            pl.BlockSpec(memory_space=pltpu.SMEM),
            pl.BlockSpec((rows, 1), lambda i: (0, 0)),
            pl.BlockSpec((STEP, 2, 2, rows, part), lambda i: (i, 0, 0, 0, 0)),
            pl.BlockSpec((STEP, 16, part), lambda i: (i, 0, 0)),
            pl.BlockSpec((STEP // group, part, group * 2 * levels), lambda i: (i, 0, 0)),
            pl.BlockSpec((rows, 2 * lats, 2 * STEP), lambda i: (0, 0, i)),
        ],
        out_specs=[
            pl.BlockSpec((lats * 4 * rows, LANES), lambda i: (0, 0)),
            pl.BlockSpec((STEP, 16, LANES), lambda i: (i, 0, 0)),
        ],
        out_shape=[
            jax.ShapeDtypeStruct((lats * 4 * rows, LANES), jnp.float32),
            jax.ShapeDtypeStruct((units, 16, LANES), jnp.float32),
        ],
        scratch_shapes=[
            pltpu.VMEM((2, rows * 2 * STEP, LANES), jnp.float32),
            pltpu.VMEM((rows, 2, 2 * lats, LANES), jnp.float32),
        ],
        compiler_params=pltpu.CompilerParams(vmem_limit_bytes=56 * 1024 * 1024),
        cost_estimate=pl.CostEstimate(
            flops=units * rows * 4 * part * levels * 3, bytes_accessed=units * rows * 1024,
            transcendentals=0),
    )(ids, low, x, xd, w, tables)


def gathered_matrices(matrices, part):
    units, _, levels, _ = matrices.shape
    group = 2 if units % 2 == 0 else 1
    count = lax.axis_size("lev")
    turned = matrices.transpose(0, 3, 1, 2).reshape(units // group, group, count, part, 2 * levels)
    turned = turned.transpose(2, 0, 3, 1, 4)
    turned = turned.reshape(count, units // group, part, group * 2 * levels)
    if count == 2:
        lev = lax.axis_index("lev")
        kept = jnp.where(lev == 0, turned[0], turned[1])
        given = jnp.where(lev == 0, turned[1], turned[0])
        taken = lax.ppermute(given, "lev", [(0, 1), (1, 0)])
        both = jnp.stack([jnp.where(lev == 0, kept, taken), jnp.where(lev == 0, taken, kept)])
    else:
        both = lax.all_to_all(turned, "lev", split_axis=0, concat_axis=0, tiled=True)
    both = both.reshape(count * (units // group), part, group * 2 * levels)
    return lax.all_gather(both, "wave", axis=0, tiled=True)


def body(spec_main, spec_diag, pair_slots, correlation, balance, legendre, legendre_diag):
    part = spec_main.shape[1]
    slots = spec_main.shape[2]
    pairs = spec_main.shape[3] // 4
    here = correlation.shape[0]
    levels = correlation.shape[-1]
    lats = legendre.shape[1]
    shared = here % 2 == 0
    half = here // 2 if shared else here
    owners = pairs // here
    rows = -(-slots // 16) * 16
    fld = lax.axis_index("fld")

    own = correlation[:, :, 0]
    combined = jnp.einsum(
        "bskl,bslm->bskm", balance, own, preferred_element_type=jnp.float32
    ).astype(jnp.bfloat16)
    coupling = combined
    if shared:
        moved = lax.ppermute(combined[half:], "fld", [(0, 1)])
        coupling = jnp.where(fld == 0, combined[:half], moved)
    w_own = gathered_matrices(own, part)
    w_coupled = gathered_matrices(coupling, part)

    spec, diag = spec_main[0], spec_diag[0]
    other, other_diag = spec, diag
    if shared:
        other, other_diag = lax.ppermute((spec, diag), "fld", [(0, 1)])

    def halves(value, width):
        return value.reshape(value.shape[:-1] + (owners, 2, half * width))

    def chosen(mine, given, width):
        if not shared:
            return mine
        first = halves(mine, width)[..., 0, :]
        second = halves(given, width)[..., 1, :]
        picked = jnp.where(fld == 0, first, second)
        return picked.reshape(picked.shape[:-2] + (owners * half * width,))

    def entries(value):
        units = value.shape[-1] // 4
        turned = value.transpose(2, 1, 0).reshape(units, 2, 2, slots, part)
        return jnp.pad(turned, ((0, 0), (0, 0), (0, 0), (0, rows - slots), (0, 0)))

    pair_ids = jnp.arange(pairs, dtype=jnp.int32)
    half_ids = chosen(pair_ids, pair_ids, 1)

    def diag_entries(value, ids):
        onehot = (pair_slots[:, None] == ids[None, :]).astype(jnp.bfloat16)
        found = jnp.einsum(
            "krc,rb->bck", value.reshape(part, slots, 2), onehot,
            preferred_element_type=jnp.float32
        ).astype(jnp.bfloat16)
        return jnp.pad(found, ((0, 0), (0, 14), (0, 0)))

    low = jnp.pad(pair_slots, (0, rows - slots))[:, None]
    columns = jnp.arange(2 * pairs, dtype=jnp.int32)
    second = (columns % 2 == 1)[None, None, :]
    lower = (columns // 2)[None, None, :] >= pair_slots[:, None, None]
    nothing = jnp.zeros_like(legendre)
    tables = jnp.concatenate(
        [jnp.where(~second | lower, legendre, nothing),
         jnp.where(second & ~lower, legendre, nothing)], axis=1)
    tables = jnp.pad(tables, ((0, rows - slots), (0, 0), (0, 0)))
    half_tables = chosen(tables, tables, 2)

    own_orders = jnp.stack([pair_slots, NWAVE - 1 - pair_slots], axis=1)
    fourier_table = order_table(own_orders, NLON).reshape(slots * 4, NLON)
    fourier_table = jnp.pad(fourier_table, ((0, 4 * (rows - slots)), (0, 0)))

    def on_grid(ids, x, xd, w, table):
        coeffs, sector = synthesize(ids, low, x, xd, w, table, levels)
        picked = (pair_slots[:, None] == ids[None, :])
        at_slot = jnp.einsum(
            "rb,bck->rck", picked.astype(jnp.float32), sector[:, :2, :levels],
            precision=lax.Precision.HIGH, preferred_element_type=jnp.float32)
        at_slot = jnp.pad(at_slot, ((0, rows - slots), (0, 0), (0, 0)))
        sect_p = jnp.pad(legendre_diag.astype(jnp.float32), ((0, rows - slots), (0, 0)))
        extra = sect_p.T[:, :, None, None] * at_slot[None]
        extra = jnp.stack([jnp.zeros_like(extra), extra], axis=2)
        coeffs = coeffs.reshape(lats, 4 * rows, LANES)[:, :, :levels]
        coeffs = coeffs + extra.reshape(lats, 4 * rows, levels)
        return jnp.einsum("jqk,ql->jkl", coeffs, fourier_table,
                          precision=lax.Precision.HIGH, preferred_element_type=jnp.float32)

    grid_own = on_grid(pair_ids, entries(spec), diag_entries(diag, pair_ids), w_own, tables)
    x_half = entries(chosen(spec, other, 4))
    diag_half = jnp.where(fld == 0, diag, other_diag)
    grid_coupled = on_grid(
        half_ids, x_half, diag_entries(diag_half, half_ids), w_coupled, half_tables)
    arrived = lax.ppermute(grid_coupled, "fld", [(0, 1)])
    if shared:
        arrived = arrived + grid_coupled
    total = grid_own + jnp.where(fld == 0, 0.0, arrived)
    banded = lax.psum_scatter(total, "lev", scatter_dimension=1, tiled=True)
    banded = lax.psum_scatter(banded, "wave", scatter_dimension=0, tiled=True)
    return banded.transpose(1, 0, 2)[None]


def solution(mesh):
    return jax.shard_map(
        body,
        mesh=mesh,
        in_specs=(
            P(("members", "fld"), "lev", "wave", None),
            P(("members", "fld"), "lev", "wave"),
            P("wave"),
            P(("wave", "lev"), None, "fld", None, None),
            P(("wave", "lev"), None, None, None),
            P("wave", None, None),
            P("wave", None),
        ),
        out_specs=P(("members", "fld"), "lev", "wave", None),
        check_vma=False,
    )
```

time: 1710 us -> 828 us (0.48)
  blocking collectives: 1110 us -> 0 us
  Pallas kernels: 0 us -> 317 us
  waiting for transfers between devices: 186 us -> 66.1 us
  matrix products: 102 us -> 26.7 us
  other arithmetic: 9.3 us -> 72.2 us
  local copies, waits for them, and re-layouts: 260 us -> 303 us
    all_to_all x2 -> x0, blocking collectives: 842 us -> none  [the longest x1 421 us: body(): lax.all_to_all(spec_main, 'wave', split_axis=3, concat_axis=2, tiled=True)]
    pallas_call x0 -> x2, Pallas kernels: none -> 317 us  [synthesize(): pl.pallas_call(functools.partial(synth_kernel, group, rows, levels, lats)...]
    all_gather x2 -> x0, blocking collectives: 260 us -> none  [the longest x1 229 us: body(): lax.all_gather(spec_diag, ('wave', 'lev'), axis=0, tiled=True)]
    all_to_all x7 -> x0, local copies, waits for them, and re-layouts: 159 us -> none  [the longest x3 56.1 us: body(): lax.all_to_all(spec_main, 'wave', split_axis=3, concat_axis=2, tiled=True)]
    all_to_all x2 -> x0, waiting for transfers between devices: 145 us -> none  [the longest x1 145 us: body(): lax.all_to_all(lax.all_to_all(spec_main, 'wave', split_axis=3, concat_axi...]
    select_n x0 -> x12, local copies, waits for them, and re-layouts: none -> 83.4 us  [the longest x3 70.5 us: chosen(): picked = jnp.where(fld == 0, first, second)]
    dot_general x10 -> x7, matrix products: 102 us -> 26.7 us  [the longest x2 21.9 us: on_grid(): jnp.einsum('jqk,ql->jkl', coeffs, fourier_table, precision=lax.Precision....]
    transpose x2 -> x4, local copies, waits for them, and re-layouts: 0.49 us -> 70.4 us  [the longest x1 62.6 us: entries(): turned = value.transpose(2, 1, 0).reshape(units, 2, 2, slots, part)]
  transfers between devices with their start and end apart: 5 -> 10, of which waited for: 3 -> 4; matrix products, arithmetic and copies ran while one was open for 2% -> 45% of each run, Pallas kernels for 0% -> 25%
where the time goes in v1:
time: 828 us; the launch traced here: 818 us
  Pallas kernels  317 us (38%)
  local copies, waits for them, and re-layouts  303 us (37%)
  other arithmetic  72.2 us (9%)
  waiting for transfers between devices  66.1 us (8%)
  matrix products  26.7 us (3%)
  starting transfers between devices  18.9 us (2%)
  between operations  13.7 us (2%)
    pallas_call x2, Pallas kernels, synthesize(): pl.pallas_call(functools.partial(synth_kernel, group, rows, levels, lats)...  317 us
    select_n x3, local copies, waits for them, and re-layouts, chosen(): picked = jnp.where(fld == 0, first, second)  70.5 us
    transpose x1, local copies, waits for them, and re-layouts, entries(): turned = value.transpose(2, 1, 0).reshape(units, 2, 2, slots, part)  62.6 us
    another operation x1, local copies, waits for them, and re-layouts, halves(): return value.reshape(value.shape[:-1] + (owners, 2, half * width))  55.3 us
    reshape x1, local copies, waits for them, and re-layouts, halves(): return value.reshape(value.shape[:-1] + (owners, 2, half * width))  55.2 us
    select_n x3, other arithmetic, chosen(): picked = jnp.where(fld == 0, first, second)  43.3 us
    reduce_scatter x1, waiting for transfers between devices, body(): banded = lax.psum_scatter(total, 'lev', scatter_dimension=1, tiled=True)  27.6 us
    reduce_scatter x1, waiting for transfers between devices, body(): banded = lax.psum_scatter(banded, 'wave', scatter_dimension=0, tiled=True)  25.6 us
  transfers between devices with their start and end apart: 10, of which 4 were waited for; matrix products, arithmetic and copies ran while one was open for 45% of the time, Pallas kernels for 25%

profile of v1, /device:TPU:0, one launch (start us, length us, event | category | flops | bytes accessed | tf_op | source)
XLA Modules:
  0.0 818.0 jit_solution(14948455063140003836)
XLA Ops:
  6.5 7.5 collective-permute-start.1
  14.0 6.3 copy.153
  20.3 5.9 reshape.310
  26.2 1.8 broadcast_select_fusion.4
  28.0 2.2 copy.155
  30.1 3.8 select_n.185
  33.9 2.3 collective-permute-start
  36.2 2.2 copy.154
  38.4 3.0 select_n.183
  41.4 9.3 %collective-permute-done = bf16[24,48,384]{2,1,0:T(8,128)(2,1)} collective-permute-done((bf16[24,48,384]{2,1,0:T(8,128)(2,1)}, bf16[24,48,384]{2,1,0:T(8,128)(2,1)}, u32[]{:S(2)}, u32[]{:S(2)}) %collective-permute-start) | collective-permute-done | bytes 884768 | tf_op jit(solution)/shard_map/ppermute | solution.py:126
  50.8 1.3 select_bitcast_fusion.1
  52.1 1.4 pad_maximum_fusion.1
  53.6 1.9 collective-permute-start.2
  55.5 2.4 fusion.6
  58.0 1.4 copy-done.2
  59.5 2.8 collective-permute-start.3
  62.3 55.3 %reshape_squeeze.7 = bf16[48,96,8,2,96]{4,3,2,1,0:T(2,128)(2,1)} reshape(bf16[1,48,96,1536]{3,2,1,0:T(8,128)(2,1)} %param.7) | data formatting | bytes 28311552 | tf_op jit(solution)/shard_map/reshape;squeeze | solution.py:164
  117.6 1.5 copy.150
  119.0 0.7 copy.156.low_ref
  119.8 0.5 cosine_multiply_fusion
  120.3 0.8 copy.161
  121.4 3.2 broadcast_select_fusion.2
  124.7 4.1 pad_maximum_fusion.p_ref
  128.8 15.3 %copy.170 = bf16[96,64,768]{0,2,1:T(8,128)(2,1)} copy(bf16[96,64,768]{2,1,0:T(8,128)(2,1)} %pad_maximum_fusion.p_ref) | data formatting | bytes 18874368 | tf_op jit(solution)/shard_map/concatenate | solution.py:195
  144.1 8.2 %slice_select_fusion = bf16[96,64,8,1,48]{0,4,3,2,1:T(8,128)(2,1)} fusion(bf16[96,64,8,2,48]{0,4,3,2,1:T(8,128)(2,1)} %bitcast.75, pred[]{:T(512)S(6)} %eq.49), kind=kLoop, calls=%fused_computation.2 | loop fusion | flops 2359296 | bytes 14155777 | tf_op jit(solution)/shard_map/jit(_where)/select_n | solution.py:171
  152.3 8.5 %copy.172.p_ref = bf16[96,64,384]{2,1,0:T(8,128)(2,1)} copy(bf16[96,64,384]{0,2,1:T(8,128)(2,1)} %bitcast.76) | data formatting | bytes 9437184 | tf_op jit(solution)/shard_map/jit(_where)/select_n | solution.py:171
  160.8 0.7 copy.158
  161.5 62.6 %copy.149 = bf16[1536,96,48]{2,1,0:T(8,128)(2,1)} copy(bf16[1536,96,48]{0,1,2:T(8,128)(2,1)} %bitcast.74) | data formatting | bytes 28311552 | tf_op jit(solution)/shard_map/transpose | solution.py:176
  224.1 1.7 convolution_convert_fusion
  225.8 1.7 copy.152
  227.5 2.4 pad.10.xd_ref
  230.1 0.9 copy.167
  230.9 0.7 reshape.324
  231.8 0.5 copy.169
  232.3 0.3 select_n.210
  232.6 1.8 collective-permute-start.4
  234.4 0.7 broadcast_select_fusion.7
  235.3 0.2 convolution_convert_fusion.1
  235.6 1.1 pad.11.xd_ref
  236.7 0.5 copy.168
  237.2 0.3 select_n.208
  237.5 3.4 collective-permute-done.4
  241.1 1.0 pad_maximum_fusion.2
  242.2 0.5 iota.41.ids_ref
  242.7 207.1 %shard_map.73 = (f32[12288,128]{1,0:T(8,128)}, f32[384,16,128]{2,1,0:T(8,128)}) custom-call(s32[384]{0:T(512)} %iota.41.ids_ref, s32[96,1]{1,0:T(8,128)} %copy.156.low_ref, bf16[384,2,2,96,48]{4,3,2,1,0:T(8,128)(2,1)} %bitcast.71, bf16[384,16,48]{2,1,0:T(8,128)(2,1)} %pad.10.xd_ref, bf16[192,48,384]{2,1,0:T(8,128)(2,1)} %all-gather.3.cloned.1.call-done.w_ref, ...), custom_call_target="tpu_custom_call" | custom-call | flops 2038431744 | bytes 37748736 | tf_op jit(solution)/shard_map/pallas_call | solution.py:85
  449.8 1.5 slice.59
  451.3 0.3 fusion.10
  451.6 55.2 %reshape.321 = bf16[48,96,8,2,96]{4,3,2,1,0:T(2,128)(2,1)} reshape(bf16[48,96,1536]{2,1,0:T(8,128)(2,1)} %collective-permute-done.1) | data formatting | bytes 28311552 | tf_op jit(solution)/shard_map/reshape | solution.py:164
  506.8 35.1 %broadcast_select_fusion = bf16[48,96,8,1,96]{4,3,2,1,0:T(2,128)(2,1)} fusion(pred[]{:T(512)S(6)} %eq.49, bf16[48,96,8,2,96]{4,3,2,1,0:T(2,128)(2,1)} %reshape.321, bf16[48,96,8,2,96]{4,3,2,1,0:T(2,128)(2,1)} %reshape_squeeze.7), kind=kLoop, calls=%fused_computation | loop fusion | flops 3538944 | bytes 21233664 | tf_op jit(solution)/shard_map/jit(_where)/select_n | solution.py:171
  541.9 61.9 %copy.163 = bf16[48,96,8,1,96]{0,1,4,2,3:T(8,128)(2,1)} copy(bf16[48,96,8,1,96]{4,3,2,1,0:T(2,128)(2,1)} %broadcast_select_fusion) | data formatting | bytes 14155776 | tf_op jit(solution)/shard_map/jit(_where)/select_n | solution.py:171
  603.9 110.0 %shard_map.74 = (f32[12288,128]{1,0:T(8,128)}, f32[192,16,128]{2,1,0:T(8,128)}) custom-call(s32[192]{0:T(256)} %copy-done.7, s32[96,1]{1,0:T(8,128)} %copy.156.low_ref, bf16[192,2,2,96,48]{4,3,2,1,0:T(8,128)(2,1)} %bitcast.72, bf16[192,16,48]{2,1,0:T(8,128)(2,1)} %pad.11.xd_ref, bf16[96,48,384]{2,1,0:T(8,128)(2,1)} %all-gather.5.cloned.1.call-done.w_ref, ...), custom_call_target="tpu_custom_call" | custom-call | flops 1019215872 | bytes 18874368 | tf_op jit(solution)/shard_map/pallas_call | solution.py:85
  713.9 1.2 slice.71
  715.1 0.2 fusion.13
  715.4 0.9 broadcast_multiply_fusion
  716.3 1.1 stack.48
  717.4 6.6 copy_add_fusion
  724.0 9.0 %fusion = f32[32,96,128]{2,1,0:T(8,128)} fusion(f32[384,128,1]{1,0,2:T(8,128)S(1)} %bitcast.84, f32[32,384,96]{2,0,1:T(8,128)S(1)} %copy_add_fusion), kind=kOutput, calls=%fused_computation.5 | convolution fusion | flops 905969664 | bytes 6488064 | tf_op jit(solution)/shard_map/jqk,ql->jkl/dot_general | solution.py:217
  733.0 2.5 collective-permute-start.5
  735.5 1.1 stack.41
  736.5 6.7 copy_add_fusion.1
  743.3 12.9 %select_add_fusion = f32[32,96,128]{2,1,0:T(8,128)} fusion(f32[32,96,128]{2,1,0:T(8,128)} %collective-permute-done.5, f32[32,96,128]{2,1,0:T(8,128)} %fusion, pred[]{:T(512)S(6)} %eq.49, f32[384,128,1]{1,0,2:T(8,128)S(1)} %bitcast.85, f32[32,384,96]{2,0,1:T(8,128)S(1)} %copy_add_fusion.1), kind=kOutput, calls=%fused_computation.15 | convolution fusion | flops 907149312 | bytes 9633793 | tf_op jit(solution)/shard_map/jqk,ql->jkl/dot_general | solution.py:217
  756.3 27.6 %reduce-scatter.3.cloned.1.call-done = f32[32,48,128]{2,1,0:T(8,128)} async-done(((f32[32,96,128]{2,1,0:T(8,128)}), f32[32,48,128]{2,1,0:T(8,128)}) %reduce-scatter.3.cloned.1.call-update) | async-done | bytes 786448 | tf_op jit(solution)/shard_map/reduce_scatter | solution.py:229
  784.0 25.6 %reduce-scatter.5.cloned.1.call-done = f32[8,48,128]{2,1,0:T(8,128)} async-done(((f32[32,48,128]{2,1,0:T(8,128)}), f32[8,48,128]{2,1,0:T(8,128)}) %reduce-scatter.5.cloned.1.call-update) | async-done | bytes 196624 | tf_op jit(solution)/shard_map/reduce_scatter | solution.py:230
  809.5 1.7 copy.177
  (52 shorter events, 1.4 us)
Async XLA Ops:
  6.5 49.0 %copy-start = (bf16[48,2,96,96]{3,2,1,0:T(8,128)(2,1)S(1)}, bf16[48,2,96,96]{3,2,1,0:T(8,128)(2,1)}, u32[]{:S(2)}) copy-start(bf16[48,2,96,96]{3,2,1,0:T(8,128)(2,1)} %param.11) | copy-start | bytes 5308420
  6.5 235.6 %all-gather.3.cloned.1.call-start = ((), (), s32[]{:S(2)}) async-start(), calls=%async_computation.2 | async-start | bytes 8847360 | tf_op jit(solution)/shard_map/all_gather | solution.py:131
  6.5 445.1 %collective-permute-start.1 = (bf16[48,96,1536]{2,1,0:T(8,128)(2,1)}, bf16[48,96,1536]{2,1,0:T(8,128)(2,1)}, u32[]{:S(2)}, u32[]{:S(2)}) collective-permute-start(bf16[48,96,1536]{2,1,0:T(8,128)(2,1)} %bitcast.73), channel_id=1, source_target_pairs={{0,1},{2,3},{4,5},{6,7},{8,9},{10,11},{12,13},{14,15},{16,17},{18,... | collective-permute-start | bytes 42467336 | tf_op jit(solution)/shard_map/ppermute | solution.py:161
  33.9 16.9 %collective-permute-start = (bf16[24,48,384]{2,1,0:T(8,128)(2,1)}, bf16[24,48,384]{2,1,0:T(8,128)(2,1)}, u32[]{:S(2)}, u32[]{:S(2)}) collective-permute-start(bf16[24,48,384]{2,1,0:T(8,128)(2,1)} %select_n.185), channel_id=1, source_target_pairs={{0,2},{2,0},{1,3},{3,1},{4,6},{6,4},{5,7},{7,5},{8,10},{10,8},{9,1... | collective-permute-start | bytes 2654216 | tf_op jit(solution)/shard_map/ppermute | solution.py:126
  53.6 550.3 %all-gather.5.cloned.1.call-start = ((), (), s32[]{:S(2)}) async-start(), calls=%async_computation.3 | async-start | bytes 4423680 | tf_op jit(solution)/shard_map/all_gather | solution.py:131
  53.6 180.8 %collective-permute-start.2 = (bf16[48,192]{1,0:T(8,128)(2,1)}, bf16[48,192]{1,0:T(8,128)(2,1)}, u32[]{:S(2)}, u32[]{:S(2)}) collective-permute-start(bf16[48,192]{1,0:T(8,128)(2,1)} %bitcast.23), channel_id=1, source_target_pairs={{0,1},{2,3},{4,5},{6,7},{8,9},{10,11},{12,13},{14,15},{16,17},{18,... | collective-permute-start | bytes 55304 | tf_op jit(solution)/shard_map/ppermute | solution.py:161
  58.0 1.4 copy-start.2
  59.5 170.4 %collective-permute-start.3 = (bf16[24,2,96,96]{3,2,1,0:T(8,128)(2,1)S(1)}, bf16[24,2,96,96]{3,2,1,0:T(8,128)(2,1)}, u32[]{:S(2)}, u32[]{:S(2)}) collective-permute-start(bf16[24,2,96,96]{3,2,1,0:T(8,128)(2,1)S(1)} %slice.80), channel_id=1, source_target_pairs={{0,1},{2,3},{4,5},{6,7},{8,9},{10,11},{12,13},{14,15},{16,17},{18,... | collective-permute-start | bytes 2654216 | tf_op jit(solution)/shard_map/ppermute | solution.py:153
  62.3 56.7 %copy-start.6 = (s32[96]{0:T(128)S(1)}, s32[96]{0:T(128)}, u32[]{:S(2)}) copy-start(s32[96]{0:T(128)} %param.9) | copy-start | bytes 1156
  121.2 114.0 %copy-start.7 = (s32[192]{0:T(256)}, s32[192]{0:T(256)S(1)}, u32[]{:S(2)}) copy-start(s32[192]{0:T(256)S(1)} %select_n.197.ids_ref) | copy-start | bytes 2308
  152.3 8.5 %copy-start.9 = (bf16[96,32]{0,1:T(8,128)(2,1)S(1)}, bf16[96,32]{0,1:T(8,128)(2,1)}, u32[]{:S(2)}) copy-start(bf16[96,32]{0,1:T(8,128)(2,1)} %param.13) | copy-start | bytes 18436
  161.5 68.4 %copy-start.3 = (bf16[48,2,96,96]{3,2,1,0:T(8,128)(2,1)S(1)}, bf16[48,2,96,96]{3,2,1,0:T(8,128)(2,1)}, u32[]{:S(2)}) copy-start(bf16[48,2,96,96]{3,2,1,0:T(8,128)(2,1)} %copy-done.2) | copy-start | bytes 5308420
  232.6 8.4 %collective-permute-start.4 = (bf16[12,48,384]{2,1,0:T(8,128)(2,1)S(1)}, bf16[12,48,384]{2,1,0:T(8,128)(2,1)S(1)}, u32[]{:S(2)}, u32[]{:S(2)}) collective-permute-start(bf16[12,48,384]{2,1,0:T(8,128)(2,1)S(1)} %select_n.210), channel_id=1, source_target_pairs={{0,2},{2,0},{1,3},{3,1},{4,6},{6,4},{5,7},{7,5},{8,10},{10,8},{9,1... | collective-permute-start | bytes 1327112 | tf_op jit(solution)/shard_map/ppermute | solution.py:126
  242.1 541.8 %reduce-scatter.3.cloned.1.call-start = ((), (), s32[]{:S(2)}) async-start(), calls=%async_computation.4 | async-start | bytes 2359296 | tf_op jit(solution)/shard_map/reduce_scatter | solution.py:229
  603.8 111.2 %copy-start.8 = (s32[192]{0:T(256)S(1)}, s32[192]{0:T(256)}, u32[]{:S(2)}) copy-start(s32[192]{0:T(256)} %copy-done.7) | copy-start | bytes 2308
  603.8 111.6 %copy-start.5 = (f32[32,96]{0,1:T(8,128)S(1)}, f32[32,96]{0,1:T(8,128)}, u32[]{:S(2)}) copy-start(f32[32,96]{0,1:T(8,128)} %copy.158) | copy-start | bytes 36868
  717.4 6.6 copy-start.4
  733.0 10.3 %collective-permute-start.5 = (f32[32,96,128]{2,1,0:T(8,128)}, f32[32,96,128]{2,1,0:T(8,128)}, u32[]{:S(2)}, u32[]{:S(2)}) collective-permute-start(f32[32,96,128]{2,1,0:T(8,128)} %fusion), channel_id=1, source_target_pairs={{0,1},{2,3},{4,5},{6,7},{8,9},{10,11},{12,13},{14,15},{16,17},{18,... | collective-permute-start | bytes 4718600 | tf_op jit(solution)/shard_map/ppermute | solution.py:225
  736.5 74.7 %copy-start.1 = (bf16[48,2,96,96]{3,2,1,0:T(8,128)(2,1)S(1)}, bf16[48,2,96,96]{3,2,1,0:T(8,128)(2,1)}, u32[]{:S(2)}) copy-start(bf16[48,2,96,96]{3,2,1,0:T(8,128)(2,1)} %param.11) | copy-start | bytes 5308420
  756.2 53.3 %reduce-scatter.5.cloned.1.call-start = ((), (), s32[]{:S(2)}) async-start(), calls=%async_computation.5 | async-start | bytes 983040 | tf_op jit(solution)/shard_map/reduce_scatter | solution.py:230
Sparse Core Ops, SparseCore 0:
  53.7 129.7 all-gather.2
  242.2 71.4 all-gather.4
  756.4 27.5 reduce-scatter.2
  786.2 23.3 reduce-scatter.4

commit v2 on v1

--- a/solution.py
+++ b/solution.py
@@ -22,74 +22,132 @@
     return jnp.stack([weight * jnp.cos(angles), -weight * jnp.sin(angles)], axis=-2)
 
 
-def synth_kernel(group, rows, levels, lats, ids_ref, low_ref, x_ref, xd_ref, w_ref, p_ref,
+def turn_kernel(part, rows, blocks, count, half, fld_ref, x_ref, xd_ref, out_ref, wide, turned):
+    pitch = rows + 8
+    for block in range(blocks):
+        for k in range(part):
+            wide[k * pitch:k * pitch + rows] = (
+                x_ref[k, :, block * LANES:(block + 1) * LANES].astype(jnp.float32))
+
+        def slot(g, carry, block=block):
+            found = [wide[pl.ds(g * 16 + i, part, stride=pitch), :].T for i in range(16)]
+            for i in range(16):
+                turned[pl.ds(block * LANES * pitch + g * 16 + i, LANES, stride=pitch), 0:part] = found[i]
+            return carry
+
+        lax.fori_loop(0, rows // 16, slot, 0)
+
+    def unit(g, carry):
+        for i in range(2):
+            u = g * 2 + i
+            source = u if half is None else (u // half * 2 + fld_ref[0]) * half + u % half
+            for q in range(4):
+                start = pl.multiple_of((source * 4 + q) * pitch, 8)
+                out_ref[u, q * rows:(q + 1) * rows, :] = (
+                    turned[pl.ds(start, rows), :].astype(jnp.bfloat16))
+            out_ref[u, 4 * rows:, 0:part] = xd_ref[u]
+        return carry
+
+    lax.fori_loop(0, count // 2, unit, 0)
+
+
+def turn(fld, value, xd, half):
+    part, rows, columns = value.shape
+    lanes = LANES if half is None else 4 * 4 * half
+    count = lanes // 4 if half is None else lanes // 8
+    pitch = rows + 8
+    return pl.pallas_call(
+        functools.partial(turn_kernel, part, rows, lanes // LANES, count, half),
+        grid=(columns // lanes,),
+        in_specs=[
+            pl.BlockSpec(memory_space=pltpu.SMEM),
+            pl.BlockSpec((part, rows, lanes), lambda i: (0, 0, i)),
+            pl.BlockSpec((count, 16, part), lambda i: (i, 0, 0)),
+        ],
+        out_specs=pl.BlockSpec((count, 4 * rows + 16, LANES), lambda i: (i, 0, 0)),
+        out_shape=jax.ShapeDtypeStruct(
+            (columns // lanes * count, 4 * rows + 16, LANES), jnp.bfloat16),
+        scratch_shapes=[
+            pltpu.VMEM((part * pitch, LANES), jnp.float32),
+            pltpu.VMEM((lanes * pitch, LANES), jnp.float32),
+        ],
+        compiler_params=pltpu.CompilerParams(vmem_limit_bytes=56 * 1024 * 1024),
+        cost_estimate=pl.CostEstimate(
+            flops=0, bytes_accessed=100 * 1024 * 1024, transcendentals=0),
+    )(fld, value, xd)
+
+
+def synth_kernel(group, rows, levels, part, lats, ids_ref, low_ref, x_ref, w_ref, p_ref,
                  out_ref, diag_ref, ysc, acc):
     step = pl.program_id(0)
     steps = pl.num_programs(0)
+    pitch = 2 * STEP + 8
     orders = jnp.concatenate([low_ref[...], low_ref[...]], axis=0)
-
-    def unit_group(g, carry):
-        for e in range(group):
-            u = g * group + e
-            w = w_ref[g]
-            base = e * 2 * levels
-            w_low = w[:, base:base + levels]
-            w_up = w[:, base + levels:base + 2 * levels]
-            first = x_ref[u, 0].reshape(2 * rows, x_ref.shape[-1])
-            second = x_ref[u, 1].reshape(2 * rows, x_ref.shape[-1])
-            y0 = jnp.dot(first, w_up, preferred_element_type=jnp.float32)
-            y1u = jnp.dot(second, w_up, preferred_element_type=jnp.float32)
-            y1l = jnp.dot(second, w_low, preferred_element_type=jnp.float32)
-            diag_ref[u, :, 0:levels] = jnp.dot(xd_ref[u], w_up, preferred_element_type=jnp.float32)
+    gap = jnp.zeros((part, LANES - levels), jnp.bfloat16)
+
+    def units(g, carry):
+        for e in range(16):
+            u = g * 16 + e
+            w = w_ref[g * (16 // group) + e // group]
+            base = e % group * 2 * levels
+            both = jnp.concatenate(
+                [w[:, base + levels:base + 2 * levels], gap, w[:, base:base + levels], gap], axis=1)
+            y = jnp.dot(x_ref[u, :, 0:part], both, preferred_element_type=jnp.float32)
             b = ids_ref[step * STEP + u]
-            y1 = jnp.where(orders <= b, y1l, y1u)
+            y1 = jnp.where(orders <= b, y[2 * rows:4 * rows, LANES:], y[2 * rows:4 * rows, :LANES])
+            diag_ref[u] = y[4 * rows:, :LANES]
             for c in range(2):
-                for s, y in ((0, y0), (1, y1)):
-                    ysc[c, pl.ds(2 * u + s, rows, stride=2 * STEP), 0:levels] = (
-                        y[c * rows:(c + 1) * rows])
+                ysc[c, pl.ds(2 * u, rows, stride=pitch), :] = y[c * rows:(c + 1) * rows, :LANES]
+                ysc[c, pl.ds(2 * u + 1, rows, stride=pitch), :] = y1[c * rows:(c + 1) * rows]
         return carry
 
-    lax.fori_loop(0, STEP // group, unit_group, 0)
+    lax.fori_loop(0, STEP // 16, units, 0)
 
     @pl.when(step == 0)
     def _():
         acc[...] = jnp.zeros_like(acc)
 
-    def slot(r, carry):
-        start = pl.multiple_of(r * 2 * STEP, 2 * STEP)
-        table = p_ref[r]
-        for c in range(2):
-            y = ysc[c, pl.ds(start, 2 * STEP), :].astype(jnp.bfloat16)
-            acc[r, c] += jnp.dot(table, y, preferred_element_type=jnp.float32)
+    def slots(g, carry):
+        sums = []
+        for i in range(8):
+            start = pl.multiple_of((g * 8 + i) * pitch, 8)
+            y = jnp.concatenate(
+                [ysc[c, pl.ds(start, 2 * STEP), :].astype(jnp.bfloat16) for c in range(2)], axis=1)
+            sums.append(jnp.dot(p_ref[g * 8 + i], y, preferred_element_type=jnp.float32))
+        for i in range(8):
+            acc[g * 8 + i] += sums[i]
         return carry
 
-    lax.fori_loop(0, rows, slot, 0)
+    lax.fori_loop(0, rows // 8, slots, 0)
 
     @pl.when(step == steps - 1)
     def _():
-        def spread(r, carry):
-            for c in range(2):
-                for i in range(2):
-                    out_ref[pl.ds(r * 4 + i * 2 + c, lats, stride=4 * rows), :] = (
-                        acc[r, c, i * lats:(i + 1) * lats])
+        def spread(g, carry):
+            for e in range(4):
+                r = g * 4 + e
+                for c in range(2):
+                    for i in range(2):
+                        out_ref[pl.ds(r * 4 + i * 2 + c, lats, stride=4 * rows), :] = (
+                            acc[r, i * lats:(i + 1) * lats, c * LANES:(c + 1) * LANES])
             return carry
 
-        lax.fori_loop(0, rows, spread, 0)
-
-
-def synthesize(ids, low, x, xd, w, tables, levels):
-    units, _, _, rows, part = x.shape
+        lax.fori_loop(0, rows // 4, spread, 0)
+
+
+def synthesize(ids, low, x, w, tables, levels):
+    units, depth, _ = x.shape
+    rows = tables.shape[0]
+    part = w.shape[1]
     lats = tables.shape[1] // 2
     group = w.shape[-1] // (2 * levels)
     steps = units // STEP
     return pl.pallas_call(
-        functools.partial(synth_kernel, group, rows, levels, lats),
+        functools.partial(synth_kernel, group, rows, levels, part, lats),
         grid=(steps,),
         in_specs=[
             pl.BlockSpec(memory_space=pltpu.SMEM),
             pl.BlockSpec((rows, 1), lambda i: (0, 0)),
-            pl.BlockSpec((STEP, 2, 2, rows, part), lambda i: (i, 0, 0, 0, 0)),
-            pl.BlockSpec((STEP, 16, part), lambda i: (i, 0, 0)),
+            pl.BlockSpec((STEP, depth, LANES), lambda i: (i, 0, 0)),
             pl.BlockSpec((STEP // group, part, group * 2 * levels), lambda i: (i, 0, 0)),
             pl.BlockSpec((rows, 2 * lats, 2 * STEP), lambda i: (0, 0, i)),
         ],
@@ -102,14 +160,14 @@
             jax.ShapeDtypeStruct((units, 16, LANES), jnp.float32),
         ],
         scratch_shapes=[
-            pltpu.VMEM((2, rows * 2 * STEP, LANES), jnp.float32),
-            pltpu.VMEM((rows, 2, 2 * lats, LANES), jnp.float32),
-        ],
-        compiler_params=pltpu.CompilerParams(vmem_limit_bytes=56 * 1024 * 1024),
+            pltpu.VMEM((2, rows * (2 * STEP + 8), LANES), jnp.float32),
+            pltpu.VMEM((rows, 2 * lats, 2 * LANES), jnp.float32),
+        ],
+        compiler_params=pltpu.CompilerParams(vmem_limit_bytes=60 * 1024 * 1024),
         cost_estimate=pl.CostEstimate(
-            flops=units * rows * 4 * part * levels * 3, bytes_accessed=units * rows * 1024,
+            flops=units * rows * 4 * part * levels * 3, bytes_accessed=units * rows * 2048,
             transcendentals=0),
-    )(ids, low, x, xd, w, tables)
+    )(ids, low, x, w, tables)
 
 
 def gathered_matrices(matrices, part):
@@ -138,7 +196,7 @@
     here = correlation.shape[0]
     levels = correlation.shape[-1]
     lats = legendre.shape[1]
-    shared = here % 2 == 0
+    shared = here % 16 == 0
     half = here // 2 if shared else here
     owners = pairs // here
     rows = -(-slots // 16) * 16
@@ -171,11 +229,6 @@
         picked = jnp.where(fld == 0, first, second)
         return picked.reshape(picked.shape[:-2] + (owners * half * width,))
 
-    def entries(value):
-        units = value.shape[-1] // 4
-        turned = value.transpose(2, 1, 0).reshape(units, 2, 2, slots, part)
-        return jnp.pad(turned, ((0, 0), (0, 0), (0, 0), (0, rows - slots), (0, 0)))
-
     pair_ids = jnp.arange(pairs, dtype=jnp.int32)
     half_ids = chosen(pair_ids, pair_ids, 1)
 
@@ -202,8 +255,8 @@
     fourier_table = order_table(own_orders, NLON).reshape(slots * 4, NLON)
     fourier_table = jnp.pad(fourier_table, ((0, 4 * (rows - slots)), (0, 0)))
 
-    def on_grid(ids, x, xd, w, table):
-        coeffs, sector = synthesize(ids, low, x, xd, w, table, levels)
+    def on_grid(ids, x, w, table):
+        coeffs, sector = synthesize(ids, low, x, w, table, levels)
         picked = (pair_slots[:, None] == ids[None, :])
         at_slot = jnp.einsum(
             "rb,bck->rck", picked.astype(jnp.float32), sector[:, :2, :levels],
@@ -217,18 +270,25 @@
         return jnp.einsum("jqk,ql->jkl", coeffs, fourier_table,
                           precision=lax.Precision.HIGH, preferred_element_type=jnp.float32)
 
-    grid_own = on_grid(pair_ids, entries(spec), diag_entries(diag, pair_ids), w_own, tables)
-    x_half = entries(chosen(spec, other, 4))
-    diag_half = jnp.where(fld == 0, diag, other_diag)
-    grid_coupled = on_grid(
-        half_ids, x_half, diag_entries(diag_half, half_ids), w_coupled, half_tables)
+    place = fld.astype(jnp.int32).reshape(1)
+    padded = jnp.pad(spec, ((0, 0), (0, rows - slots), (0, 0)))
+    x_own = turn(place, padded, diag_entries(diag, pair_ids), None)
+    x_half = x_own
+    if shared:
+        source = jnp.where(fld == 0, spec, other)
+        diag_half = jnp.where(fld == 0, diag, other_diag)
+        source = jnp.pad(source, ((0, 0), (0, rows - slots), (0, 0)))
+        x_half = turn(place, source, diag_entries(diag_half, half_ids), half)
+    grid_own = on_grid(pair_ids, x_own, w_own, tables)
+    grid_coupled = on_grid(half_ids, x_half, w_coupled, half_tables)
     arrived = lax.ppermute(grid_coupled, "fld", [(0, 1)])
     if shared:
         arrived = arrived + grid_coupled
     total = grid_own + jnp.where(fld == 0, 0.0, arrived)
-    banded = lax.psum_scatter(total, "lev", scatter_dimension=1, tiled=True)
-    banded = lax.psum_scatter(banded, "wave", scatter_dimension=0, tiled=True)
-    return banded.transpose(1, 0, 2)[None]
+    wave_count, lev_count = lax.axis_size("wave"), lax.axis_size("lev")
+    total = total.reshape(wave_count, lats // wave_count, lev_count, part, NLON)
+    total = total.transpose(0, 2, 3, 1, 4).reshape(owners, part, lats // wave_count, NLON)
+    return lax.psum_scatter(total, ("wave", "lev"), scatter_dimension=0, tiled=True)
 
 
 def solution(mesh):

time: 828 us -> 442 us (0.53)
  local copies, waits for them, and re-layouts: 303 us -> 64.6 us
  Pallas kernels: 317 us -> 158 us
  waiting for transfers between devices: 66.1 us -> 105 us
  other arithmetic: 72.2 us -> 50.6 us
    pallas_call x2 -> x4, Pallas kernels: 317 us -> 158 us  [the longest x2 89.5 us: synthesize(): pl.pallas_call(functools.partial(synth_kernel, group, rows, levels, part,...]
    select_n x3 -> x2, local copies, waits for them, and re-layouts: 70.5 us -> 8.58 us  [chosen(): picked = jnp.where(fld == 0, first, second)]
    transpose x1, local copies, waits for them, and re-layouts: 62.6 us -> 2.11 us  [body(): total.transpose(0, 2, 3, 1, 4)]
    another operation x1 -> x0, local copies, waits for them, and re-layouts: 55.3 us -> none  [halves(): return value.reshape(value.shape[:-1] + (owners, 2, half * width))]
    reshape x1 -> x0, local copies, waits for them, and re-layouts: 55.2 us -> none  [halves(): return value.reshape(value.shape[:-1] + (owners, 2, half * width))]
    select_n x3 -> x2, other arithmetic: 43.3 us -> 8.24 us  [chosen(): picked = jnp.where(fld == 0, first, second)]
    all_gather x2, waiting for transfers between devices: 0.02 us -> 33.6 us  [gathered_matrices(): return lax.all_gather(both, 'wave', axis=0, tiled=True)]
    select_n x0 -> x1, other arithmetic: none -> 13 us  [body(): source = jnp.where(fld == 0, spec, other)]
  transfers between devices with their start and end apart: 10 -> 9, of which waited for: 4 -> 3; matrix products, arithmetic and copies ran while one was open for 45% -> 20% of each run, Pallas kernels for 25% -> 28%
where the time goes in v2:
time: 442 us; the launch traced here: 434 us
  Pallas kernels  158 us (36%)
  waiting for transfers between devices  105 us (24%)
  local copies, waits for them, and re-layouts  64.6 us (15%)
  other arithmetic  50.6 us (11%)
  starting transfers between devices  21.7 us (5%)
  matrix products  20.3 us (5%)
  between operations  13.7 us (3%)
    pallas_call x2, Pallas kernels, synthesize(): pl.pallas_call(functools.partial(synth_kernel, group, rows, levels, part,...  89.5 us
    pallas_call x2, Pallas kernels, turn(): pl.pallas_call(functools.partial(turn_kernel, part, rows, lanes // LANES,...  68.4 us
    reduce_scatter x1, waiting for transfers between devices, body(): lax.psum_scatter(total, ('wave', 'lev'), scatter_dimension=0, tiled=True)  63.2 us
    all_gather x2, waiting for transfers between devices, gathered_matrices(): return lax.all_gather(both, 'wave', axis=0, tiled=True)  33.6 us
    dot_general x2, matrix products, on_grid(): jnp.einsum('jqk,ql->jkl', coeffs, fourier_table, precision=lax.Precision....  17 us
    concatenate x1, local copies, waits for them, and re-layouts, body(): jnp.concatenate([jnp.where(~second | lower, legendre, nothing), jnp.where...  15.3 us
    add x2, other arithmetic, on_grid(): coeffs = coeffs + extra.reshape(lats, 4 * rows, levels)  13.2 us
    select_n x1, other arithmetic, body(): source = jnp.where(fld == 0, spec, other)  13 us
  transfers between devices with their start and end apart: 9, of which 3 were waited for; matrix products, arithmetic and copies ran while one was open for 20% of the time, Pallas kernels for 28%

profile of v2, /device:TPU:0, one launch (start us, length us, event | category | flops | bytes accessed | tf_op | source)
XLA Modules:
  0.0 434.0 jit_solution(6439121437049331661)
XLA Ops:
  6.5 6.4 %copy.142 = bf16[48,96,2,96]{3,2,1,0:T(2,128)(2,1)} copy(bf16[48,96,2,96]{1,3,2,0:T(8,128)(2,1)} %bitcast.68) | data formatting | bytes 3538944 | tf_op jit(solution)/shard_map/transpose | solution.py:177
  13.0 5.9 %reshape.305 = bf16[24,2,2,48,192]{4,3,2,1,0:T(8,128)(2,1)} reshape(bf16[48,96,2,96]{3,2,1,0:T(2,128)(2,1)} %copy.142) | data formatting | bytes 3538944 | tf_op jit(solution)/shard_map/reshape | solution.py:177
  18.9 1.8 broadcast_select_fusion.4
  20.6 2.2 copy.144
  22.8 3.8 select_n.181
  26.6 2.9 collective-permute-start
  29.5 6.5 %collective-permute-start.1 = (bf16[48,96,1536]{2,1,0:T(8,128)(2,1)}, bf16[48,96,1536]{2,1,0:T(8,128)(2,1)}, u32[]{:S(2)}, u32[]{:S(2)}) collective-permute-start(bf16[48,96,1536]{2,1,0:T(8,128)(2,1)} %bitcast.64), channel_id=1, source_target_pairs={{0,1},{2,3},{4,5},{6,7},{8,9},{10,11},{12,13},{14,15},{16,17},{18,... | collective-permute-start | bytes 42467336 | tf_op jit(solution)/shard_map/ppermute | solution.py:219
  36.0 2.2 copy.143
  38.2 3.0 select_n.179
  41.2 8.3 %collective-permute-done = bf16[24,48,384]{2,1,0:T(8,128)(2,1)} collective-permute-done((bf16[24,48,384]{2,1,0:T(8,128)(2,1)}, bf16[24,48,384]{2,1,0:T(8,128)(2,1)}, u32[]{:S(2)}, u32[]{:S(2)}) %collective-permute-start) | collective-permute-done | bytes 884768 | tf_op jit(solution)/shard_map/ppermute | solution.py:184
  49.5 1.3 select_bitcast_fusion.1
  50.8 1.5 pad_maximum_fusion.1
  52.4 2.4 fusion.6
  54.8 1.4 copy-done.2
  56.3 2.3 collective-permute-start.3
  58.6 2.0 collective-permute-start.2
  60.7 0.2 compare_or_fusion
  60.9 3.8 broadcast_select_fusion.2
  64.7 4.1 pad_maximum_fusion.p_ref
  68.8 0.1 fusion.9
  68.9 0.9 copy.155
  69.8 0.7 reshape.317
  70.7 0.5 copy.157
  71.2 0.3 select_n.205
  71.5 1.8 collective-permute-start.4
  73.3 0.8 copy.139
  74.2 15.3 %copy.158 = bf16[96,64,768]{0,2,1:T(8,128)(2,1)} copy(bf16[96,64,768]{2,1,0:T(8,128)(2,1)} %pad_maximum_fusion.p_ref) | data formatting | bytes 18874368 | tf_op jit(solution)/shard_map/concatenate | solution.py:248
  89.5 0.5 copy.156
  90.1 0.3 select_n.203
  90.5 1.0 pad_maximum_fusion.2
  91.6 0.5 cosine_multiply_fusion
  92.1 0.2 convolution_convert_fusion
  92.4 8.2 %slice_select_fusion = bf16[96,64,8,1,48]{0,4,3,2,1:T(8,128)(2,1)} fusion(bf16[96,64,8,2,48]{0,4,3,2,1:T(8,128)(2,1)} %bitcast.66, pred[]{:T(512)S(6)} %eq.49), kind=kLoop, calls=%fused_computation.2 | loop fusion | flops 2359296 | bytes 14155777 | tf_op jit(solution)/shard_map/jit(_where)/select_n | solution.py:229
  100.6 0.7 copy.145.low_ref
  101.4 8.5 %copy.160.p_ref = bf16[96,64,384]{2,1,0:T(8,128)(2,1)} copy(bf16[96,64,384]{0,2,1:T(8,128)(2,1)} %bitcast.67) | data formatting | bytes 9437184 | tf_op jit(solution)/shard_map/jit(_where)/select_n | solution.py:229
  109.9 0.2 copy.141
  110.2 0.2 copy.150
  110.3 1.5 pad.10.xd_ref
  111.8 34.4 %shard_map.73.x_ref = bf16[384,400,128]{2,1,0:T(8,128)(2,1)} custom-call(s32[1]{0:T(128)} %bitcast.1.fld_ref, bf16[48,96,1536]{2,1,0:T(8,128)(2,1)} %bitcast.65, bf16[384,16,48]{2,1,0:T(8,128)(2,1)} %pad.10.xd_ref), custom_call_target="tpu_custom_call" | custom-call | bytes 104857600 | tf_op jit(solution)/shard_map/pallas_call | solution.py:59
  146.3 0.7 broadcast_select_fusion.7
  147.0 0.1 copy.152
  147.1 0.2 convolution_convert_fusion.1
  147.3 0.1 copy.154
  147.5 1.1 pad.11.xd_ref
  148.5 33.6 %all-gather.3.cloned.1.call-done.w_ref = bf16[192,48,384]{2,1,0:T(8,128)(2,1)} async-done(((bf16[48,48,384]{2,1,0:T(8,128)(2,1)}), bf16[192,48,384]{2,1,0:T(8,128)(2,1)}) %all-gather.3.cloned.1.call-update) | async-done | bytes 7077904 | tf_op jit(solution)/shard_map/all_gather | solution.py:189
  182.2 0.6 iota.41.ids_ref
  182.8 55.1 %shard_map.74 = (f32[12288,128]{1,0:T(8,128)}, f32[384,16,128]{2,1,0:T(8,128)}) custom-call(s32[384]{0:T(512)} %iota.41.ids_ref, s32[96,1]{1,0:T(8,128)} %copy.145.low_ref, bf16[384,400,128]{2,1,0:T(8,128)(2,1)} %shard_map.73.x_ref, bf16[192,48,384]{2,1,0:T(8,128)(2,1)} %all-gather.3.cloned.1.call-done.w_ref, bf16[96,64,768]{2,1,0:T(8,128)(2,1)} %pad_maximum_fusion.p_ref), custom_call_target="tpu_custom_call" | custom-call | flops 2038431744 | bytes 75497472 | tf_op jit(solution)/shard_map/pallas_call | solution.py:144
  237.9 1.5 slice.53
  239.4 0.3 fusion.10
  239.8 13.0 %broadcast_select_fusion.x_ref = bf16[48,96,1536]{2,1,0:T(8,128)(2,1)} fusion(bf16[48,96,1536]{2,1,0:T(8,128)(2,1)} %collective-permute-done.1, pred[]{:T(512)S(6)} %eq.49, bf16[1,48,96,1536]{3,2,1,0:T(8,128)(2,1)} %param.7), kind=kLoop, calls=%fused_computation | loop fusion | flops 7077888 | bytes 42467328 | tf_op jit(solution)/shard_map/jit(_where)/select_n | solution.py:278
  252.7 34.0 %shard_map.75.x_ref = bf16[192,400,128]{2,1,0:T(8,128)(2,1)} custom-call(s32[1]{0:T(128)} %bitcast.1.fld_ref, bf16[48,96,1536]{2,1,0:T(8,128)(2,1)} %broadcast_select_fusion.x_ref, bf16[192,16,48]{2,1,0:T(8,128)(2,1)} %pad.11.xd_ref), custom_call_target="tpu_custom_call" | custom-call | bytes 104857600 | tf_op jit(solution)/shard_map/pallas_call | solution.py:59
  286.8 34.4 %shard_map.76 = (f32[12288,128]{1,0:T(8,128)}, f32[192,16,128]{2,1,0:T(8,128)}) custom-call(s32[192]{0:T(256)} %copy-done.7, s32[96,1]{1,0:T(8,128)} %copy.145.low_ref, bf16[192,400,128]{2,1,0:T(8,128)(2,1)} %shard_map.75.x_ref, bf16[96,48,384]{2,1,0:T(8,128)(2,1)} %all-gather.5.cloned.1.call-done.w_ref, bf16[96,64,384]{2,1,0:T(8,128)(2,1)} %copy.160.p_ref), custom_call_target="tpu_custom_call" | custom-call | flops 1019215872 | bytes 37748736 | tf_op jit(solution)/shard_map/pallas_call | solution.py:144
  321.1 1.2 slice.63
  322.3 0.2 fusion.13
  322.7 0.9 broadcast_multiply_fusion
  323.6 1.1 stack.48
  324.6 6.6 %copy_add_fusion = f32[32,384,96]{2,0,1:T(8,128)S(1)} fusion(f32[32,384,96]{2,1,0:T(8,128)} %bitcast.73, f32[32,96,2,2,96]{4,0,3,2,1:T(8,128)S(1)} %stack.48), kind=kLoop, calls=%fused_computation.3 | loop fusion | flops 1179648 | bytes 14155776 | tf_op jit(solution)/shard_map/add | solution.py:269
  331.2 7.8 %fusion = f32[32,96,128]{2,1,0:T(8,128)S(1)} fusion(f32[384,128,1]{1,0,2:T(8,128)S(1)} %bitcast.77, f32[32,384,96]{2,0,1:T(8,128)S(1)} %copy_add_fusion), kind=kOutput, calls=%fused_computation.5 | convolution fusion | flops 905969664 | bytes 6488064 | tf_op jit(solution)/shard_map/jqk,ql->jkl/dot_general | solution.py:270
  339.0 6.0 %collective-permute-start.5 = (f32[32,96,128]{2,1,0:T(8,128)S(1)}, f32[32,96,128]{2,1,0:T(8,128)}, u32[]{:S(2)}, u32[]{:S(2)}) collective-permute-start(f32[32,96,128]{2,1,0:T(8,128)S(1)} %fusion), channel_id=1, source_target_pairs={{0,1},{2,3},{4,5},{6,7},{8,9},{10,11},{12,13},{14,15},{16,17},{18,... | collective-permute-start | bytes 4718600 | tf_op jit(solution)/shard_map/ppermute | solution.py:284
  345.0 1.1 stack.41
  346.0 6.7 %copy_add_fusion.1 = f32[32,384,96]{2,0,1:T(8,128)S(1)} fusion(f32[32,384,96]{2,1,0:T(8,128)} %bitcast.72, f32[32,96,2,2,96]{4,0,3,2,1:T(8,128)S(1)} %stack.41), kind=kLoop, calls=%fused_computation.4 | loop fusion | flops 1179648 | bytes 14155776 | tf_op jit(solution)/shard_map/add | solution.py:269
  352.8 9.2 %select_add_fusion = f32[32,96,128]{2,1,0:T(8,128)S(1)} fusion(f32[32,96,128]{2,1,0:T(8,128)} %collective-permute-done.5, f32[32,96,128]{2,1,0:T(8,128)S(1)} %copy-done.5, pred[]{:T(512)S(6)} %eq.49, f32[384,128,1]{1,0,2:T(8,128)S(1)} %bitcast.78, f32[32,384,96]{2,0,1:T(8,128)S(1)} %copy_add_fusion.1), kind=kOutput, calls=%fused_computation.15 | convolution fusion | flops 907149312 | bytes 9633793 | tf_op jit(solution)/shard_map/jqk,ql->jkl/dot_general | solution.py:270
  362.0 2.1 copy.165
  364.1 63.2 %reduce-scatter.2.cloned.1.call-done = f32[1,48,8,128]{3,2,1,0:T(8,128)} async-done(((f32[8,48,8,128]{3,2,1,0:T(8,128)}), f32[1,48,8,128]{3,2,1,0:T(8,128)}) %reduce-scatter.2.cloned.1.call-update) | async-done | bytes 196624 | tf_op jit(solution)/shard_map/reduce_scatter | solution.py:291
  (47 shorter events, 0.8 us)
Async XLA Ops:
  6.5 45.8 %copy-start = (bf16[48,2,96,96]{3,2,1,0:T(8,128)(2,1)S(1)}, bf16[48,2,96,96]{3,2,1,0:T(8,128)(2,1)}, u32[]{:S(2)}) copy-start(bf16[48,2,96,96]{3,2,1,0:T(8,128)(2,1)} %param.11) | copy-start | bytes 5308420
  6.5 175.7 %all-gather.3.cloned.1.call-start = ((), (), s32[]{:S(2)}) async-start(), calls=%async_computation.1 | async-start | bytes 8847360 | tf_op jit(solution)/shard_map/all_gather | solution.py:189
  26.6 22.9 %collective-permute-start = (bf16[24,48,384]{2,1,0:T(8,128)(2,1)}, bf16[24,48,384]{2,1,0:T(8,128)(2,1)}, u32[]{:S(2)}, u32[]{:S(2)}) collective-permute-start(bf16[24,48,384]{2,1,0:T(8,128)(2,1)} %select_n.181), channel_id=1, source_target_pairs={{0,2},{2,0},{1,3},{3,1},{4,6},{6,4},{5,7},{7,5},{8,10},{10,8},{9,1... | collective-permute-start | bytes 2654216 | tf_op jit(solution)/shard_map/ppermute | solution.py:184
  29.5 210.2 %collective-permute-start.1 = (bf16[48,96,1536]{2,1,0:T(8,128)(2,1)}, bf16[48,96,1536]{2,1,0:T(8,128)(2,1)}, u32[]{:S(2)}, u32[]{:S(2)}) collective-permute-start(bf16[48,96,1536]{2,1,0:T(8,128)(2,1)} %bitcast.64), channel_id=1, source_target_pairs={{0,1},{2,3},{4,5},{6,7},{8,9},{10,11},{12,13},{14,15},{16,17},{18,... | collective-permute-start | bytes 42467336 | tf_op jit(solution)/shard_map/ppermute | solution.py:219
  52.3 8.4 %copy-start.6 = (s32[96]{0:T(128)S(1)}, s32[96]{0:T(128)}, u32[]{:S(2)}) copy-start(s32[96]{0:T(128)} %param.9) | copy-start | bytes 1156
  52.3 234.4 %all-gather.5.cloned.1.call-start = ((), (), s32[]{:S(2)}) async-start(), calls=%async_computation.2 | async-start | bytes 4423680 | tf_op jit(solution)/shard_map/all_gather | solution.py:189
  54.8 1.4 copy-start.2
  56.3 12.5 %collective-permute-start.3 = (bf16[24,2,96,96]{3,2,1,0:T(8,128)(2,1)S(1)}, bf16[24,2,96,96]{3,2,1,0:T(8,128)(2,1)}, u32[]{:S(2)}, u32[]{:S(2)}) collective-permute-start(bf16[24,2,96,96]{3,2,1,0:T(8,128)(2,1)S(1)} %slice.70), channel_id=1, source_target_pairs={{0,1},{2,3},{4,5},{6,7},{8,9},{10,11},{12,13},{14,15},{16,17},{18,... | collective-permute-start | bytes 2654216 | tf_op jit(solution)/shard_map/ppermute | solution.py:211
  58.6 87.6 %collective-permute-start.2 = (bf16[48,192]{1,0:T(8,128)(2,1)}, bf16[48,192]{1,0:T(8,128)(2,1)}, u32[]{:S(2)}, u32[]{:S(2)}) collective-permute-start(bf16[48,192]{1,0:T(8,128)(2,1)} %bitcast.19), channel_id=1, source_target_pairs={{0,1},{2,3},{4,5},{6,7},{8,9},{10,11},{12,13},{14,15},{16,17},{18,... | collective-permute-start | bytes 55304 | tf_op jit(solution)/shard_map/ppermute | solution.py:219
  64.7 4.1 copy-start.3
  71.5 18.9 %collective-permute-start.4 = (bf16[12,48,384]{2,1,0:T(8,128)(2,1)S(1)}, bf16[12,48,384]{2,1,0:T(8,128)(2,1)S(1)}, u32[]{:S(2)}, u32[]{:S(2)}) collective-permute-start(bf16[12,48,384]{2,1,0:T(8,128)(2,1)S(1)} %select_n.205), channel_id=1, source_target_pairs={{0,2},{2,0},{1,3},{3,1},{4,6},{6,4},{5,7},{7,5},{8,10},{10,8},{9,1... | collective-permute-start | bytes 1327112 | tf_op jit(solution)/shard_map/ppermute | solution.py:184
  90.1 2.0 copy-start.9
  91.5 335.8 %reduce-scatter.2.cloned.1.call-start = ((), (), s32[]{:S(2)}) async-start(), calls=%async_computation.3 | async-start | bytes 1769472 | tf_op jit(solution)/shard_map/reduce_scatter | solution.py:291
  101.4 45.7 %copy-start.7 = (s32[192]{0:T(256)}, s32[192]{0:T(256)S(1)}, u32[]{:S(2)}) copy-start(s32[192]{0:T(256)S(1)} %select_n.193.ids_ref) | copy-start | bytes 2308
  286.8 35.6 %copy-start.8 = (s32[192]{0:T(256)S(1)}, s32[192]{0:T(256)}, u32[]{:S(2)}) copy-start(s32[192]{0:T(256)} %copy-done.7) | copy-start | bytes 2308
  339.0 7.1 %copy-start.4 = (f32[32,96,128]{2,1,0:T(8,128)}, f32[32,96,128]{2,1,0:T(8,128)S(1)}, u32[]{:S(2)}) copy-start(f32[32,96,128]{2,1,0:T(8,128)S(1)} %fusion) | copy-start | bytes 4718596
  339.0 13.8 %collective-permute-start.5 = (f32[32,96,128]{2,1,0:T(8,128)S(1)}, f32[32,96,128]{2,1,0:T(8,128)}, u32[]{:S(2)}, u32[]{:S(2)}) collective-permute-start(f32[32,96,128]{2,1,0:T(8,128)S(1)} %fusion), channel_id=1, source_target_pairs={{0,1},{2,3},{4,5},{6,7},{8,9},{10,11},{12,13},{14,15},{16,17},{18,... | collective-permute-start | bytes 4718600 | tf_op jit(solution)/shard_map/ppermute | solution.py:284
  346.0 6.7 %copy-start.5 = (f32[32,96,128]{2,1,0:T(8,128)S(1)}, f32[32,96,128]{2,1,0:T(8,128)}, u32[]{:S(2)}) copy-start(f32[32,96,128]{2,1,0:T(8,128)} %copy-done.4) | copy-start | bytes 4718596
  352.7 74.6 %copy-start.1 = (bf16[48,2,96,96]{3,2,1,0:T(8,128)(2,1)S(1)}, bf16[48,2,96,96]{3,2,1,0:T(8,128)(2,1)}, u32[]{:S(2)}) copy-start(bf16[48,2,96,96]{3,2,1,0:T(8,128)(2,1)} %param.11) | copy-start | bytes 5308420
Sparse Core Ops, SparseCore 0:
  52.4 129.7 all-gather.2
  183.8 68.1 all-gather.4
  364.2 63.0 reduce-scatter.1

commit v3 on v2

--- a/solution.py
+++ b/solution.py
@@ -241,15 +241,17 @@
         return jnp.pad(found, ((0, 0), (0, 14), (0, 0)))
 
     low = jnp.pad(pair_slots, (0, rows - slots))[:, None]
-    columns = jnp.arange(2 * pairs, dtype=jnp.int32)
-    second = (columns % 2 == 1)[None, None, :]
-    lower = (columns // 2)[None, None, :] >= pair_slots[:, None, None]
-    nothing = jnp.zeros_like(legendre)
-    tables = jnp.concatenate(
-        [jnp.where(~second | lower, legendre, nothing),
-         jnp.where(second & ~lower, legendre, nothing)], axis=1)
-    tables = jnp.pad(tables, ((0, rows - slots), (0, 0), (0, 0)))
-    half_tables = chosen(tables, tables, 2)
+    def masked(values, ids):
+        second = (jnp.arange(values.shape[-1], dtype=jnp.int32) % 2 == 1)[None, None, :]
+        lower = jnp.repeat(ids, 2)[None, None, :] >= pair_slots[:, None, None]
+        nothing = jnp.zeros_like(values)
+        both = jnp.concatenate(
+            [jnp.where(~second | lower, values, nothing),
+             jnp.where(second & ~lower, values, nothing)], axis=1)
+        return jnp.pad(both, ((0, rows - slots), (0, 0), (0, 0)))
+
+    tables = masked(legendre, pair_ids)
+    half_tables = masked(chosen(legendre, legendre, 2), half_ids) if shared else tables
 
     own_orders = jnp.stack([pair_slots, NWAVE - 1 - pair_slots], axis=1)
     fourier_table = order_table(own_orders, NLON).reshape(slots * 4, NLON)
@@ -279,16 +281,22 @@
         diag_half = jnp.where(fld == 0, diag, other_diag)
         source = jnp.pad(source, ((0, 0), (0, rows - slots), (0, 0)))
         x_half = turn(place, source, diag_entries(diag_half, half_ids), half)
+        x_own, x_half = lax.optimization_barrier((x_own, x_half))
     grid_own = on_grid(pair_ids, x_own, w_own, tables)
     grid_coupled = on_grid(half_ids, x_half, w_coupled, half_tables)
     arrived = lax.ppermute(grid_coupled, "fld", [(0, 1)])
     if shared:
         arrived = arrived + grid_coupled
     total = grid_own + jnp.where(fld == 0, 0.0, arrived)
-    wave_count, lev_count = lax.axis_size("wave"), lax.axis_size("lev")
-    total = total.reshape(wave_count, lats // wave_count, lev_count, part, NLON)
-    total = total.transpose(0, 2, 3, 1, 4).reshape(owners, part, lats // wave_count, NLON)
-    return lax.psum_scatter(total, ("wave", "lev"), scatter_dimension=0, tiled=True)
+    if lax.axis_size("lev") == 2:
+        lev = lax.axis_index("lev")
+        kept = jnp.where(lev == 0, total[:, :part], total[:, part:])
+        given = jnp.where(lev == 0, total[:, part:], total[:, :part])
+        banded = kept + lax.ppermute(given, "lev", [(0, 1), (1, 0)])
+    else:
+        banded = lax.psum_scatter(total, "lev", scatter_dimension=1, tiled=True)
+    banded = lax.psum_scatter(banded, "wave", scatter_dimension=0, tiled=True)
+    return banded.transpose(1, 0, 2)[None]
 
 
 def solution(mesh):

time: 442 us -> 388 us (0.88)
  waiting for transfers between devices: 105 us -> 71.7 us
  local copies, waits for them, and re-layouts: 64.6 us -> 43.8 us
    reduce_scatter x1, waiting for transfers between devices: 63.2 us -> 21.7 us  [body(): banded = lax.psum_scatter(banded, 'wave', scatter_dimension=0, tiled=True)]
    all_gather x2, waiting for transfers between devices: 33.6 us -> 13.6 us  [gathered_matrices(): return lax.all_gather(both, 'wave', axis=0, tiled=True)]
    ppermute x0 -> x1, waiting for transfers between devices: none -> 16.2 us  [body(): banded = kept + lax.ppermute(given, 'lev', [(0, 1), (1, 0)])]
    concatenate x1 -> x0, local copies, waits for them, and re-layouts: 15.3 us -> none  [body(): jnp.concatenate([jnp.where(~second | lower, legendre, nothing), jnp.where...]
    ppermute x2, waiting for transfers between devices: 8.26 us -> 20.2 us  [gathered_matrices(): taken = lax.ppermute(given, 'lev', [(0, 1), (1, 0)])]
    unnamed x21 -> x28, local copies, waits for them, and re-layouts: 2.3 us -> 12.2 us
    concatenate x1 -> x2, other arithmetic: 4.07 us -> 9.58 us  [masked(): jnp.concatenate([jnp.where(~second | lower, values, nothing), jnp.where(s...]
    select_n x2, local copies, waits for them, and re-layouts: 8.58 us -> 3.82 us  [chosen(): picked = jnp.where(fld == 0, first, second)]
  transfers between devices with their start and end apart: 9 -> 10, of which waited for: 3 -> 5; matrix products, arithmetic and copies ran while one was open for 20% -> 21% of each run, Pallas kernels for 28% -> 27%
where the time goes in v3:
time: 388 us; the launch traced here: 380 us
  Pallas kernels  158 us (41%)
  waiting for transfers between devices  71.7 us (18%)
  other arithmetic  53.8 us (14%)
  local copies, waits for them, and re-layouts  43.8 us (11%)
  matrix products  20.1 us (5%)
  starting transfers between devices  19.3 us (5%)
  between operations  13.8 us (4%)
    pallas_call x2, Pallas kernels, synthesize(): pl.pallas_call(functools.partial(synth_kernel, group, rows, levels, part,...  89.4 us
    pallas_call x2, Pallas kernels, turn(): pl.pallas_call(functools.partial(turn_kernel, part, rows, lanes // LANES,...  68.5 us
    reduce_scatter x1, waiting for transfers between devices, body(): banded = lax.psum_scatter(banded, 'wave', scatter_dimension=0, tiled=True)  21.7 us
    ppermute x2, waiting for transfers between devices, gathered_matrices(): taken = lax.ppermute(given, 'lev', [(0, 1), (1, 0)])  20.2 us
    dot_general x2, matrix products, on_grid(): jnp.einsum('jqk,ql->jkl', coeffs, fourier_table, precision=lax.Precision....  16.8 us
    ppermute x1, waiting for transfers between devices, body(): banded = kept + lax.ppermute(given, 'lev', [(0, 1), (1, 0)])  16.2 us
    all_gather x2, waiting for transfers between devices, gathered_matrices(): return lax.all_gather(both, 'wave', axis=0, tiled=True)  13.6 us
    add x2, other arithmetic, on_grid(): coeffs = coeffs + extra.reshape(lats, 4 * rows, levels)  13.2 us
  transfers between devices with their start and end apart: 10, of which 5 were waited for; matrix products, arithmetic and copies ran while one was open for 21% of the time, Pallas kernels for 27%

profile of v3, /device:TPU:0, one launch (start us, length us, event | category | flops | bytes accessed | tf_op | source)
XLA Modules:
  0.0 380.5 jit_solution(8368543592678610877)
XLA Ops:
  6.5 1.7 copy-done
  8.2 2.4 fusion.6
  10.6 1.4 copy-done.3
  12.1 2.4 collective-permute-start.3
  14.6 6.3 %collective-permute-start = (bf16[48,96,1536]{2,1,0:T(8,128)(2,1)}, bf16[48,96,1536]{2,1,0:T(8,128)(2,1)}, u32[]{:S(2)}, u32[]{:S(2)}) collective-permute-start(bf16[48,96,1536]{2,1,0:T(8,128)(2,1)} %bitcast.63), channel_id=1, source_target_pairs={{0,1},{2,3},{4,5},{6,7},{8,9},{10,11},{12,13},{14,15},{16,17},{18,... | collective-permute-start | bytes 42467336 | tf_op jit(solution)/shard_map/ppermute | solution.py:219
  20.9 1.4 fusion.9
  22.3 0.9 copy.159
  23.2 0.7 reshape.401
  24.0 0.5 copy.161
  24.5 1.1 select_n.230
  25.6 2.3 collective-permute-start.4
  27.9 0.5 copy.160
  28.5 0.3 select_n.228
  28.8 6.2 %collective-permute-done.4 = bf16[12,48,384]{2,1,0:T(8,128)(2,1)} collective-permute-done((bf16[12,48,384]{2,1,0:T(8,128)(2,1)}, bf16[12,48,384]{2,1,0:T(8,128)(2,1)}, u32[]{:S(2)}, u32[]{:S(2)}) %collective-permute-start.4) | collective-permute-done | bytes 442400 | tf_op jit(solution)/shard_map/ppermute | solution.py:184
  35.0 1.1 select_bitcast_fusion.3
  36.1 1.1 pad_maximum_fusion.3
  37.3 3.9 %copy.149 = bf16[48,96,2,96]{3,2,1,0:T(2,128)(2,1)} copy(bf16[48,96,2,96]{1,3,2,0:T(8,128)(2,1)S(1)} %bitcast.69) | data formatting | bytes 3538944 | tf_op jit(solution)/shard_map/transpose | solution.py:177
  41.2 4.8 %reshape.396 = bf16[24,2,2,48,192]{4,3,2,1,0:T(8,128)(2,1)S(1)} reshape(bf16[48,96,2,96]{3,2,1,0:T(2,128)(2,1)} %copy.149) | data formatting | bytes 3538944 | tf_op jit(solution)/shard_map/reshape | solution.py:177
  46.2 1.2 copy.151
  47.3 0.6 select_n.214
  47.9 1.8 collective-permute-start.2
  49.7 1.2 copy.150
  50.9 0.6 select_n.212
  51.5 13.9 %collective-permute-done.2 = bf16[24,48,384]{2,1,0:T(8,128)(2,1)} collective-permute-done((bf16[24,48,384]{2,1,0:T(8,128)(2,1)S(1)}, bf16[24,48,384]{2,1,0:T(8,128)(2,1)}, u32[]{:S(2)}, u32[]{:S(2)}) %collective-permute-start.2) | collective-permute-done | bytes 884768 | tf_op jit(solution)/shard_map/ppermute | solution.py:184
  65.4 1.3 select_bitcast_fusion.1
  66.7 1.4 pad_maximum_fusion.2
  68.2 1.5 collective-permute-start.1
  70.2 8.3 %copy.162 = bf16[96,32,768]{0,2,1:T(8,128)(2,1)} copy(bf16[96,32,768]{2,1,0:T(8,128)(2,1)} %param.12) | data formatting | bytes 9437184 | tf_op args[5]
  78.6 4.9 %slice_select_fusion = bf16[96,32,8,1,48]{0,4,3,2,1:T(8,128)(2,1)} fusion(bf16[96,32,8,2,48]{0,4,3,2,1:T(8,128)(2,1)} %bitcast.65, pred[]{:T(512)S(6)} %eq.109), kind=kLoop, calls=%fused_computation.11 | loop fusion | flops 1179648 | bytes 7077889 | tf_op jit(solution)/shard_map/jit(_where)/select_n | solution.py:229
  83.5 3.7 copy.163
  87.6 0.2 convolution_convert_fusion
  88.0 0.5 cosine_multiply_fusion
  88.5 0.8 broadcast_select_fusion.4
  89.3 3.1 pad_maximum_fusion.1.p_ref
  92.5 0.5 slice-done.1
  93.0 3.0 broadcast_select_fusion.2
  96.0 6.5 %pad_maximum_fusion.p_ref = bf16[96,64,768]{2,1,0:T(8,128)(2,1)} fusion(bf16[96,32,768]{2,1,0:T(8,128)(2,1)} %get-tuple-element.18, bf16[96,32,768]{2,1,0:T(8,128)(2,1)S(1)} %get-tuple-element.17), kind=kLoop, calls=%fused_computation.1 | loop fusion | flops 18874368 | bytes 18874368 | tf_op jit(solution)/shard_map/concatenate | solution.py:248
  102.5 0.7 copy.152.low_ref
  103.6 1.4 pad.10.xd_ref
  105.1 34.4 %shard_map.73.x_ref = bf16[384,400,128]{2,1,0:T(8,128)(2,1)} custom-call(s32[1]{0:T(128)} %bitcast.1.fld_ref, bf16[48,96,1536]{2,1,0:T(8,128)(2,1)} %bitcast.64, bf16[384,16,48]{2,1,0:T(8,128)(2,1)} %pad.10.xd_ref), custom_call_target="tpu_custom_call" | custom-call | bytes 104857600 | tf_op jit(solution)/shard_map/pallas_call | solution.py:59
  140.0 1.1 pad.11.xd_ref
  141.1 13.0 %broadcast_select_fusion.x_ref = bf16[48,96,1536]{2,1,0:T(8,128)(2,1)} fusion(bf16[48,96,1536]{2,1,0:T(8,128)(2,1)} %collective-permute-done, pred[]{:T(512)S(6)} %eq.109, bf16[1,48,96,1536]{3,2,1,0:T(8,128)(2,1)} %param.7), kind=kLoop, calls=%fused_computation | loop fusion | flops 7077888 | bytes 42467328 | tf_op jit(solution)/shard_map/jit(_where)/select_n | solution.py:280
  154.0 34.1 %shard_map.74.x_ref = bf16[192,400,128]{2,1,0:T(8,128)(2,1)} custom-call(s32[1]{0:T(128)} %bitcast.1.fld_ref, bf16[48,96,1536]{2,1,0:T(8,128)(2,1)} %broadcast_select_fusion.x_ref, bf16[192,16,48]{2,1,0:T(8,128)(2,1)} %pad.11.xd_ref), custom_call_target="tpu_custom_call" | custom-call | bytes 104857600 | tf_op jit(solution)/shard_map/pallas_call | solution.py:59
  188.1 34.0 %shard_map.76 = (f32[12288,128]{1,0:T(8,128)}, f32[192,16,128]{2,1,0:T(8,128)}) custom-call(s32[192]{0:T(256)} %copy-done.8, s32[96,1]{1,0:T(8,128)} %copy.152.low_ref, bf16[192,400,128]{2,1,0:T(8,128)(2,1)} %shard_map.74.x_ref, bf16[96,48,384]{2,1,0:T(8,128)(2,1)} %all-gather.5.cloned.1.call-done.w_ref, bf16[96,64,384]{2,1,0:T(8,128)(2,1)} %pad_maximum_fusion.1.p_ref), custom_call_target="tpu_custom_call" | custom-call | flops 1019215872 | bytes 37748736 | tf_op jit(solution)/shard_map/pallas_call | solution.py:144
  222.1 1.2 slice.71
  223.3 0.2 fusion.13
  223.6 13.6 %all-gather.3.cloned.1.call-done.w_ref = bf16[192,48,384]{2,1,0:T(8,128)(2,1)} async-done(((bf16[48,48,384]{2,1,0:T(8,128)(2,1)}), bf16[192,48,384]{2,1,0:T(8,128)(2,1)}) %all-gather.3.cloned.1.call-update) | async-done | bytes 7077904 | tf_op jit(solution)/shard_map/all_gather | solution.py:189
  237.3 0.6 iota.45.ids_ref
  237.8 55.4 %shard_map.75 = (f32[12288,128]{1,0:T(8,128)}, f32[384,16,128]{2,1,0:T(8,128)}) custom-call(s32[384]{0:T(512)} %iota.45.ids_ref, s32[96,1]{1,0:T(8,128)} %copy.152.low_ref, bf16[384,400,128]{2,1,0:T(8,128)(2,1)} %shard_map.73.x_ref, bf16[192,48,384]{2,1,0:T(8,128)(2,1)} %all-gather.3.cloned.1.call-done.w_ref, bf16[96,64,768]{2,1,0:T(8,128)(2,1)} %pad_maximum_fusion.p_ref), custom_call_target="tpu_custom_call" | custom-call | flops 2038431744 | bytes 75497472 | tf_op jit(solution)/shard_map/pallas_call | solution.py:144
  293.2 1.5 slice.63
  294.7 0.3 fusion.10
  295.1 0.9 broadcast_multiply_fusion
  296.0 1.1 stack.48
  297.1 6.6 %copy_add_fusion = f32[32,384,96]{2,0,1:T(8,128)S(1)} fusion(f32[32,384,96]{2,1,0:T(8,128)} %bitcast.72, f32[32,96,2,2,96]{4,0,3,2,1:T(8,128)S(1)} %stack.48), kind=kLoop, calls=%fused_computation.2 | loop fusion | flops 1179648 | bytes 14155776 | tf_op jit(solution)/shard_map/add | solution.py:271
  303.6 7.6 %fusion = f32[32,96,128]{2,1,0:T(8,128)S(1)} fusion(f32[384,128,1]{1,0,2:T(8,128)S(1)} %bitcast.76, f32[32,384,96]{2,0,1:T(8,128)S(1)} %copy_add_fusion), kind=kOutput, calls=%fused_computation.4 | convolution fusion | flops 905969664 | bytes 6488064 | tf_op jit(solution)/shard_map/jqk,ql->jkl/dot_general | solution.py:272
  311.2 3.3 collective-permute-start.5
  314.6 1.1 stack.41
  315.6 6.7 %copy_add_fusion.1 = f32[32,384,96]{2,0,1:T(8,128)S(1)} fusion(f32[32,384,96]{2,1,0:T(8,128)} %bitcast.73, f32[32,96,2,2,96]{4,0,3,2,1:T(8,128)S(1)} %stack.41), kind=kLoop, calls=%fused_computation.3 | loop fusion | flops 1179648 | bytes 14155776 | tf_op jit(solution)/shard_map/add | solution.py:271
  322.4 9.2 %select_add_fusion = f32[32,96,128]{2,1,0:T(8,128)S(1)} fusion(f32[32,96,128]{2,1,0:T(8,128)} %collective-permute-done.5, f32[32,96,128]{2,1,0:T(8,128)S(1)} %copy-done.5, pred[]{:T(512)S(6)} %eq.109, f32[384,128,1]{1,0,2:T(8,128)S(1)} %bitcast.77, f32[32,384,96]{2,0,1:T(8,128)S(1)} %copy_add_fusion.1), kind=kOutput, calls=%fused_computation.18 | convolution fusion | flops 907149312 | bytes 9633793 | tf_op jit(solution)/shard_map/jqk,ql->jkl/dot_general | solution.py:272
  331.7 1.5 collective-permute-start.6
  333.2 16.2 %collective-permute-done.6 = f32[32,48,128]{2,1,0:T(8,128)S(1)} collective-permute-done((f32[32,48,128]{2,1,0:T(8,128)S(1)}, f32[32,48,128]{2,1,0:T(8,128)S(1)}, u32[]{:S(2)}, u32[]{:S(2)}) %collective-permute-start.6) | collective-permute-done | bytes 786464 | tf_op jit(solution)/shard_map/ppermute | solution.py:295
  349.4 1.0 select_add_fusion.1
  350.4 21.7 %reduce-scatter.2.cloned.1.call-done = f32[8,48,128]{2,1,0:T(8,128)} async-done(((f32[32,48,128]{2,1,0:T(8,128)}), f32[8,48,128]{2,1,0:T(8,128)}) %reduce-scatter.2.cloned.1.call-update) | async-done | bytes 196624 | tf_op jit(solution)/shard_map/reduce_scatter | solution.py:298
  372.1 1.7 copy.170
  (65 shorter events, 2.7 us)
Async XLA Ops:
  6.5 1.7 copy-start
  6.5 181.6 %all-gather.5.cloned.1.call-start = ((), (), s32[]{:S(2)}) async-start(), calls=%async_computation.2 | async-start | bytes 4423680 | tf_op jit(solution)/shard_map/all_gather | solution.py:189
  10.6 1.4 copy-start.3
  12.1 8.8 %collective-permute-start.3 = (bf16[24,2,96,96]{3,2,1,0:T(8,128)(2,1)S(1)}, bf16[24,2,96,96]{3,2,1,0:T(8,128)(2,1)S(1)}, u32[]{:S(2)}, u32[]{:S(2)}) collective-permute-start(bf16[24,2,96,96]{3,2,1,0:T(8,128)(2,1)S(1)} %slice.80), channel_id=1, source_target_pairs={{0,1},{2,3},{4,5},{6,7},{8,9},{10,11},{12,13},{14,15},{16,17},{18,... | collective-permute-start | bytes 2654216 | tf_op jit(solution)/shard_map/ppermute | solution.py:211
  14.6 126.5 %collective-permute-start = (bf16[48,96,1536]{2,1,0:T(8,128)(2,1)}, bf16[48,96,1536]{2,1,0:T(8,128)(2,1)}, u32[]{:S(2)}, u32[]{:S(2)}) collective-permute-start(bf16[48,96,1536]{2,1,0:T(8,128)(2,1)} %bitcast.63), channel_id=1, source_target_pairs={{0,1},{2,3},{4,5},{6,7},{8,9},{10,11},{12,13},{14,15},{16,17},{18,... | collective-permute-start | bytes 42467336 | tf_op jit(solution)/shard_map/ppermute | solution.py:219
  25.6 9.4 %collective-permute-start.4 = (bf16[12,48,384]{2,1,0:T(8,128)(2,1)}, bf16[12,48,384]{2,1,0:T(8,128)(2,1)}, u32[]{:S(2)}, u32[]{:S(2)}) collective-permute-start(bf16[12,48,384]{2,1,0:T(8,128)(2,1)} %select_n.230), channel_id=1, source_target_pairs={{0,2},{2,0},{1,3},{3,1},{4,6},{6,4},{5,7},{7,5},{8,10},{10,8},{9,1... | collective-permute-start | bytes 1327112 | tf_op jit(solution)/shard_map/ppermute | solution.py:184
  27.9 9.3 %copy-start.2 = (bf16[48,2,1,96,96]{4,3,2,1,0:T(8,128)(2,1)S(1)}, bf16[48,2,1,96,96]{4,3,2,1,0:T(8,128)(2,1)}, u32[]{:S(2)}) copy-start(bf16[48,2,1,96,96]{4,3,2,1,0:T(8,128)(2,1)} %param.10) | copy-start | bytes 5308420
  37.2 200.1 %all-gather.3.cloned.1.call-start = ((), (), s32[]{:S(2)}) async-start(), calls=%async_computation.1 | async-start | bytes 8847360 | tf_op jit(solution)/shard_map/all_gather | solution.py:189
  47.9 17.5 %collective-permute-start.2 = (bf16[24,48,384]{2,1,0:T(8,128)(2,1)S(1)}, bf16[24,48,384]{2,1,0:T(8,128)(2,1)}, u32[]{:S(2)}, u32[]{:S(2)}) collective-permute-start(bf16[24,48,384]{2,1,0:T(8,128)(2,1)S(1)} %select_n.214), channel_id=1, source_target_pairs={{0,2},{2,0},{1,3},{3,1},{4,6},{6,4},{5,7},{7,5},{8,10},{10,8},{9,1... | collective-permute-start | bytes 2654216 | tf_op jit(solution)/shard_map/ppermute | solution.py:184
  66.7 1.5 copy-start.6
  68.2 303.9 %reduce-scatter.2.cloned.1.call-start = ((), (), s32[]{:S(2)}) async-start(), calls=%async_computation.3 | async-start | bytes 983040 | tf_op jit(solution)/shard_map/reduce_scatter | solution.py:298
  68.2 71.3 %collective-permute-start.1 = (bf16[48,192]{1,0:T(8,128)(2,1)S(1)}, bf16[48,192]{1,0:T(8,128)(2,1)S(1)}, u32[]{:S(2)}, u32[]{:S(2)}) collective-permute-start(bf16[48,192]{1,0:T(8,128)(2,1)S(1)} %bitcast.81), channel_id=1, source_target_pairs={{0,1},{2,3},{4,5},{6,7},{8,9},{10,11},{12,13},{14,15},{16,17},{18,... | collective-permute-start | bytes 55304 | tf_op jit(solution)/shard_map/ppermute | solution.py:219
  70.0 69.6 %copy-start.8 = (s32[192]{0:T(256)}, s32[192]{0:T(256)S(1)}, u32[]{:S(2)}) copy-start(s32[192]{0:T(256)S(1)} %select_n.206.ids_ref) | copy-start | bytes 2308
  83.5 3.9 %copy-start.7 = (s32[96]{0:T(128)S(1)}, s32[96]{0:T(128)}, u32[]{:S(2)}) copy-start(s32[96]{0:T(128)} %param.9) | copy-start | bytes 1156
  83.5 4.0 %copy-start.10 = (bf16[96,32]{0,1:T(8,128)(2,1)S(1)}, bf16[96,32]{0,1:T(8,128)(2,1)}, u32[]{:S(2)}) copy-start(bf16[96,32]{0,1:T(8,128)(2,1)} %param.13) | copy-start | bytes 18436
  89.3 3.2 slice-start
  89.3 3.7 slice-start.1
  188.1 35.2 %copy-start.9 = (s32[192]{0:T(256)S(1)}, s32[192]{0:T(256)}, u32[]{:S(2)}) copy-start(s32[192]{0:T(256)} %copy-done.8) | copy-start | bytes 2308
  311.2 4.4 %copy-start.4 = (f32[32,96,128]{2,1,0:T(8,128)}, f32[32,96,128]{2,1,0:T(8,128)S(1)}, u32[]{:S(2)}) copy-start(f32[32,96,128]{2,1,0:T(8,128)S(1)} %fusion) | copy-start | bytes 4718596
  311.2 11.1 %collective-permute-start.5 = (f32[32,96,128]{2,1,0:T(8,128)S(1)}, f32[32,96,128]{2,1,0:T(8,128)}, u32[]{:S(2)}, u32[]{:S(2)}) collective-permute-start(f32[32,96,128]{2,1,0:T(8,128)S(1)} %fusion), channel_id=1, source_target_pairs={{0,1},{2,3},{4,5},{6,7},{8,9},{10,11},{12,13},{14,15},{16,17},{18,... | collective-permute-start | bytes 4718600 | tf_op jit(solution)/shard_map/ppermute | solution.py:287
  315.6 6.7 %copy-start.5 = (f32[32,96,128]{2,1,0:T(8,128)S(1)}, f32[32,96,128]{2,1,0:T(8,128)}, u32[]{:S(2)}) copy-start(f32[32,96,128]{2,1,0:T(8,128)} %copy-done.4) | copy-start | bytes 4718596
  322.3 51.4 %copy-start.1 = (bf16[48,2,96,96]{3,2,1,0:T(8,128)(2,1)S(1)}, bf16[48,2,96,96]{3,2,1,0:T(8,128)(2,1)}, u32[]{:S(2)}) copy-start(bf16[48,2,96,96]{3,2,1,0:T(8,128)(2,1)} %param.11) | copy-start | bytes 5308420
  331.7 17.7 %collective-permute-start.6 = (f32[32,48,128]{2,1,0:T(8,128)S(1)}, f32[32,48,128]{2,1,0:T(8,128)S(1)}, u32[]{:S(2)}, u32[]{:S(2)}) collective-permute-start(f32[32,48,128]{2,1,0:T(8,128)S(1)} %slice_select_fusion.2), channel_id=1, source_target_pairs={{0,2},{2,0},{1,3},{3,1},{4,6},{6,4},{5,7},{7,5},{8,10},{10,8},{9,1... | collective-permute-start | bytes 2359304 | tf_op jit(solution)/shard_map/ppermute | solution.py:295
Sparse Core Ops, SparseCore 0:
  37.3 71.4 all-gather.4
  110.4 126.7 all-gather.2
  350.5 21.4 reduce-scatter.1
